TPU v7x, 128 devices: a whole 4x4x4 slice. The times are simulated.
128 devices in a mesh: replica: 2 (over z_hi), fsdp: 64 (over x, y, z_lo, core).
Axes of the slice: x: 4, y: 4, z: 4 (z_hi: 2, z_lo: 2; z = z_hi * 2 + z_lo), core: 2. Of those that a mesh axis runs over, the one named last changes fastest.
Arguments:
- inputs: bfloat16 [2, 256, 4096], P('replica'), may hold values from -6 to 6
- cotangent: bfloat16 [2, 256, 4096], P('replica', 'fsdp'), may hold values from -6 to 6
- up_weight: bfloat16 [2, 4096, 32768], P('replica', None, 'fsdp'), may hold values from -0.09375 to 0.09375
- down_weight: bfloat16 [2, 32768, 4096], P('replica', 'fsdp'), may hold values from -0.03125 to 0.03125
- local_params: float32 [2, 16, 1048576], P('replica', None, 'fsdp'), may hold values from -6 to 6
- global_params: float32 [16, 1048576], P(None, 'fsdp'), may hold values from -6 to 6
- outer_momentum: float32 [16, 1048576], P(None, 'fsdp'), may hold values from -3 to 3
- plan: int32 [16], replicated, may hold values from 0 to 7, as said below
- fragment_id: int32 [1], replicated, may hold values from 0 to 7
Outputs:
- block_out: bfloat16 [2, 256, 4096], P('replica', 'fsdp')
- input_grad: bfloat16 [2, 256, 4096], P('replica', 'fsdp')
- up_grad: bfloat16 [2, 4096, 32768], P('replica', None, 'fsdp')
- down_grad: bfloat16 [2, 32768, 4096], P('replica', 'fsdp')
- new_global: float32 [16, 1048576], P(None, 'fsdp')
- new_momentum: float32 [16, 1048576], P(None, 'fsdp')
- merged_local: float32 [2, 16, 1048576], P('replica', None, 'fsdp')
Inputs may be any that keep to these rules, and one draw needn't show every extreme that they name: `plan`: each of the 8 fragments holds exactly 2 layers.
All inputs are finite; a program needn't handle non-finite values.
Results may differ from a plain program's by a relative error of at most 0.005.
Values may be sent and summed in bfloat16 or wider, within the bound.
A program may use at most 128 MiB of HBM per device.

v0:
```python
import jax
import jax.numpy as jnp
from jax import lax
from jax.sharding import PartitionSpec as P


def gelu_value(u):
    t = jnp.tanh(0.7978845608 * (u + 0.044715 * u * u * u))
    return 0.5 * u * (1.0 + t)


def gelu_slope(u):
    t = jnp.tanh(0.7978845608 * (u + 0.044715 * u * u * u))
    return 0.5 * (1.0 + t) + 0.5 * u * (1.0 - t * t) * 0.7978845608 * (1.0 + 3.0 * 0.044715 * u * u)


def contract_last(left, right):
    return lax.dot_general(
        left, right, (((1,), (1,)), ((), ())), preferred_element_type=jnp.float32
    )


def contract_first(left, right):
    return lax.dot_general(
        left, right, (((0,), (0,)), ((), ())), preferred_element_type=jnp.float32
    )


def on_device(
    inputs,
    cotangent,
    up_weight,
    down_weight,
    local_params,
    global_params,
    outer_momentum,
    plan,
    fragment_id,
):
    tokens_in = inputs[0]
    grad_rows = cotangent[0]
    w_up = up_weight[0]
    w_down = down_weight[0]
    pre = jnp.dot(tokens_in, w_up, preferred_element_type=jnp.float32)
    hidden = gelu_value(pre).astype(jnp.bfloat16)
    rows = hidden
    block_out = lax.psum_scatter(
        jnp.dot(rows, w_down, preferred_element_type=jnp.float32),
        "fsdp",
        scatter_dimension=0,
        tiled=True,
    ).astype(jnp.bfloat16)
    piece = lax.all_gather(grad_rows, "fsdp", axis=0, tiled=True)
    rows = hidden
    down_acc = contract_first(rows, piece)
    hidden_grad = contract_last(piece, w_down)
    hidden_grad, down_acc = (hidden_grad, down_acc)
    pre_grad = (hidden_grad * gelu_slope(pre)).astype(jnp.bfloat16)
    up_grad = contract_first(tokens_in, pre_grad).astype(jnp.bfloat16)
    down_grad = down_acc.astype(jnp.bfloat16)
    rows = pre_grad
    input_grad = lax.psum_scatter(
        contract_last(rows, w_up), "fsdp", scatter_dimension=0, tiled=True
    ).astype(jnp.bfloat16)
    replicas = lax.axis_size("replica")
    mine = local_params[0]
    selected = plan == fragment_id[0]
    total = lax.psum(mine.astype(jnp.bfloat16), "replica").astype(jnp.float32)
    delta = global_params - total / replicas
    momentum = 0.9 * outer_momentum + delta
    updated = global_params - 0.7 * (delta + 0.9 * momentum)
    keep = selected[:, None]
    new_momentum = jnp.where(keep, momentum, outer_momentum)
    new_global = jnp.where(keep, updated, global_params)
    merged = jnp.where(selected[:, None], 0.5 * mine + 0.5 * new_global, mine)
    return (
        block_out[None],
        input_grad[None],
        up_grad[None],
        down_grad[None],
        new_global,
        new_momentum,
        merged[None],
    )


def solution(mesh):
    placed = (
        P("replica", None, None),
        P("replica", "fsdp", None),
        P("replica", None, "fsdp"),
        P("replica", "fsdp", None),
        P("replica", None, "fsdp"),
        P(None, "fsdp"),
        P(None, "fsdp"),
        P(),
        P(),
    )
    return jax.shard_map(
        on_device,
        mesh=mesh,
        in_specs=placed,
        out_specs=(
            P("replica", "fsdp", None),
            P("replica", "fsdp", None),
            P("replica", None, "fsdp"),
            P("replica", "fsdp", None),
            P(None, "fsdp"),
            P(None, "fsdp"),
            P("replica", None, "fsdp"),
        ),
        check_vma=False,
    )
```

profile of v0, /device:TPU:1, one launch (start us, length us, event | category | flops | bytes accessed | tf_op | source)
XLA Modules:
  0.0 484.6 jit_solution(6209892664079362787)
XLA Ops:
  8.0 0.0 copy-start
  8.0 0.0 all-reduce.6.cloned.1.call-start
  8.1 2.2 bitcast_convert_fusion
  10.3 0.0 all-reduce.6.cloned.1.call-update
  10.3 0.0 all-gather.3.cloned.1.call-start
  10.3 1.4 copy.19
  11.8 0.0 all-gather.3.cloned.1.call-update
  11.8 0.0 copy-done
  11.8 0.0 copy-start.1
  11.8 3.6 fusion.8
  15.4 0.0 copy-done.1
  15.4 0.0 copy-start.4
  15.4 0.0 copy-start.7
  15.4 0.0 copy-start.6
  15.5 0.0 copy-start.3
  15.5 3.3 fusion.4
  18.8 0.0 copy-done.4
  19.5 0.0 copy-done.7
  19.5 0.6 dynamic-slice
  20.7 0.0 copy-done.6
  20.7 31.9 %all-reduce.6.cloned.1.call-done = bf16[16,16384]{1,0:T(8,128)(2,1)} async-done(((bf16[16,16384]{1,0:T(8,128)(2,1)}), bf16[16,16384]{1,0:T(8,128)(2,1)}) %all-reduce.6.cloned.1.call-update) | async-done | bytes 524304 | tf_op jit(solution)/shard_map/psum | solution.py:68
  52.6 0.0 copy-done.3
  52.6 3.9 fusion.25
  56.5 70.8 %all-gather.3.cloned.1.call-done = bf16[1,256,4096]{2,0,1:T(2,128)(2,1)} async-done(((bf16[1,4,4096]{2,0,1:T(2,128)(2,1)}), bf16[1,256,4096]{2,0,1:T(2,128)(2,1)}) %all-gather.3.cloned.1.call-update) | async-done | bytes 2097168 | tf_op jit(solution)/shard_map/all_gather | solution.py:53
  127.2 0.0 copy-start.2
  127.2 6.7 %fusion.19 = bf16[256,512]{1,0:T(8,128)(2,1)S(1)} fusion(bf16[1,512,4096]{2,1,0:T(8,128)(2,1)} %param.12, bf16[1,256,4096]{2,0,1:T(2,128)(2,1)} %all-gather.3.cloned.1.call-done, f32[256,512]{1,0:T(8,128)} %copy-done.4), kind=kOutput, calls=%fused_computation.18 | convolution fusion | flops 1076232192 | bytes 7077888 | tf_op jit(solution)/shard_map/dot_general | solution.py:18
  134.0 0.0 copy-done.2
  134.0 3.3 fusion.6
  137.2 3.3 fusion
  140.5 6.4 %copy.20 = bf16[1,4096,512]{2,1,0:T(8,128)(2,1)} copy(bf16[1,4096,512]{1,2,0:T(8,128)(2,1)} %fusion) | data formatting | bytes 8388608
  146.9 0.0 copy-start.5
  146.9 321.5 %all-reduce.7 = (bf16[256,4096]{1,0:T(8,128)(2,1)}, bf16[256,4096]{1,0:T(8,128)(2,1)}) all-reduce(f32[256,4096]{1,0:T(8,128)} %fusion.4, f32[256,4096]{1,0:T(8,128)} %fusion.6), channel_id=3, replica_groups=mesh['replica'=2,'fsdp'=64] {'fsdp'}, use_global_device_ids=true, to_apply=%region_0.0.clone | all-reduce | flops 2097152 | bytes 12582912
  468.4 1.5 fusion.34
  469.9 0.0 copy-done.5
  469.9 7.3 %fusion.1 = bf16[1,512,4096]{2,1,0:T(8,128)(2,1)} fusion(bf16[1,256,4096]{2,0,1:T(2,128)(2,1)} %all-gather.3.cloned.1.call-done, f32[256,512]{1,0:T(8,128)S(1)} %copy-done.5), kind=kOutput, calls=%fused_computation.3 | convolution fusion | flops 1077018624 | bytes 6815744 | tf_op jit(solution)/shard_map/dot_general | solution.py:24
  (1 shorter events, 0.0 us)
Async XLA Ops:
  8.0 3.8 copy-start
  8.0 44.6 %all-reduce.6.cloned.1.call-start = ((), (), s32[]{:S(2)}) async-start(), calls=%async_computation | async-start | bytes 1048576 | tf_op jit(solution)/shard_map/psum | solution.py:68
  10.3 116.9 %all-gather.3.cloned.1.call-start = ((), (), s32[]{:S(2)}) async-start(), calls=%async_computation.1 | async-start | bytes 4259840 | tf_op jit(solution)/shard_map/all_gather | solution.py:53
  11.8 3.6 copy-start.1
  15.4 3.4 copy-start.4
  15.4 4.0 copy-start.7
  15.4 5.3 %copy-start.6 = (s32[16]{0:T(128)S(1)}, s32[16]{0:T(128)}, u32[]{:S(2)}) copy-start(s32[16]{0:T(128)} %param.16) | copy-start | bytes 196
  15.5 37.2 %copy-start.3 = (f32[1,16,16384]{2,1,0:T(8,128)S(1)}, f32[1,16,16384]{2,1,0:T(8,128)}, u32[]{:S(2)}) copy-start(f32[1,16,16384]{2,1,0:T(8,128)} %param.13) | copy-start | bytes 3145732
  127.2 6.7 %copy-start.2 = (bf16[1,4096,512]{2,1,0:T(8,128)(2,1)S(1)}, bf16[1,4096,512]{2,1,0:T(8,128)(2,1)}, u32[]{:S(2)}) copy-start(bf16[1,4096,512]{2,1,0:T(8,128)(2,1)} %param.11) | copy-start | bytes 12582916
  146.9 323.0 %copy-start.5 = (f32[256,512]{1,0:T(8,128)S(1)}, f32[256,512]{1,0:T(8,128)}, u32[]{:S(2)}) copy-start(f32[256,512]{1,0:T(8,128)} %copy-done.4) | copy-start | bytes 1572868
Sparse Core Ops, SparseCore 0:
  11.9 40.6 all-reduce.5
Sparse Core Ops, SparseCore 1:
  13.1 114.1 all-gather.2
where the time goes:
time: 491 us; the launch traced here: 485 us
  blocking collectives  322 us (66%)
  waiting for transfers between devices  103 us (21%)
  matrix products  27.4 us (6%)
  between operations  16.9 us (3%)
  local copies, waits for them, and re-layouts  10 us (2%)
  other arithmetic  6.07 us (1%)
    unnamed x1, blocking collectives  322 us
    all_gather x1, waiting for transfers between devices, on_device(): piece = lax.all_gather(grad_rows, 'fsdp', axis=0, tiled=True)  70.8 us
    psum x1, waiting for transfers between devices, on_device(): total = lax.psum(mine.astype(jnp.bfloat16), 'replica').astype(jnp.float32)  31.9 us
    dot_general x2, matrix products, contract_first(): lax.dot_general(left, right, (((0,), (0,)), ((), ())), preferred_element_...  10.5 us
    dot_general x2, matrix products, contract_last(): lax.dot_general(left, right, (((1,), (1,)), ((), ())), preferred_element_...  9.98 us
  transfers between devices with their start and end apart: 2, of which 2 were waited for; matrix products, arithmetic and copies ran while one was open for 3% of the time, Pallas kernels for 0%

commit v1 on v0

v1 whole, which is shorter than its diff:
```python
import jax
import jax.numpy as jnp
from jax import lax
from jax.experimental import pallas as pl
from jax.experimental.pallas import tpu as pltpu
from jax.sharding import PartitionSpec as P

BF = jnp.bfloat16
F32 = jnp.float32
MESH = pl.DeviceIdType.MESH
HALF = 2048


def dot(a, b, ca, cb):
    return lax.dot_general(a, b, (((ca,), (cb,)), ((), ())), preferred_element_type=F32)


def selected_rows(plan_ref, frag_ref):
    first, last = jnp.int32(15), jnp.int32(0)
    for layer in range(16):
        hit = plan_ref[layer] == frag_ref[0]
        first = jnp.minimum(first, jnp.where(hit, layer, 15))
        last = jnp.maximum(last, jnp.where(hit, layer, 0))
    return first, last


def step_kernel(
    x_hbm, cot_hbm, wu_hbm, wd_hbm, lp_hbm, plan_ref, frag_ref,
    bo_ref, ig_ref, cot_out, hid_out, pg_out, prow_ref,
    x_v, wu, wd, lp, cot4, st, cotg, slope, hid, pg, msg, peer_msg,
    own, sb, rb, part, r1, sp, rp,
    lsem, osem, s1, q1, s3, q3, s4, q4, s0, q0, sr, qr, s2, q2, sx, qx,
):
    rep = lax.axis_index("replica")
    f = lax.axis_index("fsdp")
    x, y, z, c = f // 16, (f // 4) % 4, (f // 2) % 2, f % 2
    other = 1 - c
    lo = pl.multiple_of(c * HALF, HALF)
    hi = pl.multiple_of(other * HALF, HALF)
    ring = jnp.where(c == 0, x, y)
    plane = jnp.where(c == 0, y, x)

    def dev(xx, yy, zz, cc):
        return (rep, ((xx * 4 + yy) * 2 + zz) * 2 + cc)

    def on_ring(r):
        return (rep, jnp.where(c == 0, ((r * 4 + y) * 2 + z) * 2 + c, ((x * 4 + r) * 2 + z) * 2 + c))

    def remote(src, dst, ssem, rsem, device):
        return pltpu.make_async_remote_copy(
            src_ref=src, dst_ref=dst, send_sem=ssem, recv_sem=rsem, device_id=device, device_id_type=MESH
        )

    loads = [
        pltpu.make_async_copy(cot_hbm.at[0], cot4, lsem.at[0]),
        pltpu.make_async_copy(x_hbm.at[0], x_v, lsem.at[1]),
        pltpu.make_async_copy(wu_hbm.at[0], wu, lsem.at[2]),
        pltpu.make_async_copy(wd_hbm.at[0], wd, lsem.at[3]),
        pltpu.make_async_copy(lp_hbm.at[0], lp, lsem.at[4]),
    ]
    for load in loads:
        load.start()

    barrier = pltpu.get_barrier_semaphore()

    def greet(k, _):
        u, zz, cc = k // 4, (k // 2) % 2, k % 2

        @pl.when((u * 16 + y * 4 + zz * 2 + cc) != f)
        def _():
            pl.semaphore_signal(barrier, inc=1, device_id=dev(u, y, zz, cc), device_id_type=MESH)

        @pl.when(u != y)
        def _():
            pl.semaphore_signal(barrier, inc=1, device_id=dev(x, u, zz, cc), device_id_type=MESH)

        return 0

    lax.fori_loop(0, 16, greet, 0)
    pl.semaphore_signal(barrier, inc=1, device_id=(1 - rep, f), device_id_type=MESH)
    pl.semaphore_wait(barrier, 28)

    loads[0].wait()
    st[plane * 4 + z * 2 + c] = cot4[:, pl.ds(lo, HALF)]

    def to_core0(k):
        u, zz = k // 2, k % 2
        return remote(cot4.at[:, pl.ds(0, HALF)], st.at[y * 4 + z * 2 + c], s1.at[k], q1.at[y * 4 + z * 2 + c], dev(x, u, zz, 0))

    def to_core1(k):
        u, zz = k // 2, k % 2
        return remote(cot4.at[:, pl.ds(HALF, HALF)], st.at[x * 4 + z * 2 + c], s1.at[8 + k], q1.at[x * 4 + z * 2 + c], dev(u, y, zz, 1))

    def not_self0(k):
        return (c == 1) | (k != y * 2 + z)

    def not_self1(k):
        return (c == 0) | (k != x * 2 + z)

    def stage1(k, _):
        @pl.when(not_self0(k))
        def _():
            to_core0(k).start()

        @pl.when(not_self1(k))
        def _():
            to_core1(k).start()

        return 0

    lax.fori_loop(0, 8, stage1, 0)

    loads[4].wait()
    i0, i1 = selected_rows(plan_ref, frag_ref)
    msg[0:1, :] = lp[pl.ds(i0, 1), :].astype(BF)
    msg[1:2, :] = lp[pl.ds(i1, 1), :].astype(BF)
    swap = remote(msg, peer_msg, sx.at[0], qx.at[0], (1 - rep, f))
    swap.start()

    loads[1].wait()
    loads[2].wait()
    slope[...] = dot(x_v[...], wu[...], 1, 0)
    u = slope[...]
    t = jnp.tanh(0.7978845608 * (u + 0.044715 * u * u * u))
    hid[...] = (0.5 * u * (1.0 + t)).astype(BF)
    slope[...] = 0.5 * (1.0 + t) + 0.5 * u * (1.0 - t * t) * 0.7978845608 * (1.0 + 3.0 * 0.044715 * u * u)

    def arrive1(k, _):
        @pl.when(k != plane * 4 + z * 2 + c)
        def _():
            remote(st.at[k], st.at[k], s1.at[k], q1.at[k], dev(x, y, z, other)).wait_recv()

        return 0

    lax.fori_loop(0, 16, arrive1, 0)
    for q in range(4):
        block = jnp.concatenate([st[4 * q + j].astype(F32) for j in range(4)], axis=0).astype(BF)

        @pl.when(c == 0)
        def _():
            cotg[x, q, :, 0:HALF] = block

        @pl.when(c == 1)
        def _():
            cotg[q, y, :, HALF:] = block

    def slab0(r):
        return cotg.at[r, :, :, pl.ds(0, HALF)]

    def slab1(r):
        return cotg.at[:, r, :, pl.ds(HALF, HALF)]

    def ring_copy(slab, d):
        s = slab(ring)
        return remote(s, s, s3.at[d - 1], q3.at[d - 1], on_ring((ring + d) % 4))

    def core_copy(slab, d):
        s = slab((ring + 4 - d) % 4)
        return remote(s, s, s4.at[d], q4.at[d], dev(x, y, z, other))

    def per_core(fn):
        @pl.when(c == 0)
        def _():
            fn(slab0, slab1)

        @pl.when(c == 1)
        def _():
            fn(slab1, slab0)

    def stage2(mine, theirs):
        for d in (1, 3, 2):
            ring_copy(mine, d).start()
        core_copy(mine, 0).start()

    per_core(stage2)

    def first(n, mine_fn, theirs_fn):
        sb[n] = theirs_fn().astype(BF).reshape(4, 4, 16, HALF)
        remote(sb.at[n], rb.at[n], s0.at[n], q0.at[n], dev(x, y, z, other)).start()
        own[...] = mine_fn()

    def first_done(n):
        remote(sb.at[n], rb.at[n], s0.at[n], q0.at[n], dev(x, y, z, other)).wait_recv()
        part[n] = (own[...].reshape(4, 4, 16, HALF) + rb[n].astype(F32)).astype(BF)

    def second_copy(n, d, core):
        r = (ring + d) % 4
        src = part.at[n, r] if core == 0 else part.at[n, :, r]
        return remote(src, r1.at[n, d - 1], sr.at[n, d - 1], qr.at[n, d - 1], on_ring(r))

    def second(n):
        for core in (0, 1):
            @pl.when(c == core)
            def _():
                for d in (1, 3, 2):
                    second_copy(n, d, core).start()

    def third_copy(n, k):
        q, zz, cc = k // 4, (k // 2) % 2, k % 2
        target = (rep, jnp.where(c == 0, x * 16 + q * 4, q * 16 + y * 4) + zz * 2 + cc)
        slot = c * 8 + plane * 2 + z
        return remote(sp.at[n, k], rp.at[n, slot], s2.at[n, k], q2.at[n, slot], target)

    def second_done(n):
        for d in (1, 3, 2):
            second_copy(n, d, 0).wait_recv()
        for core in (0, 1):
            @pl.when(c == core)
            def _():
                for q in range(4):
                    mine = part[n, x, q] if core == 0 else part[n, q, y]
                    v = mine.astype(F32) + r1[n, 0, q].astype(F32) + r1[n, 1, q].astype(F32) + r1[n, 2, q].astype(F32)
                    for j in range(4):
                        sp[n, 4 * q + j] = v[4 * j : 4 * j + 4].astype(BF)

    def third(n):
        def go(k, _):
            @pl.when(k != plane * 4 + z * 2 + c)
            def _():
                third_copy(n, k).start()

            return 0

        rp[n, c * 8 + plane * 2 + z] = sp[n, plane * 4 + z * 2 + c]
        lax.fori_loop(0, 16, go, 0)

    def third_done(n, out):
        def go(k, _):
            @pl.when(k != c * 8 + plane * 2 + z)
            def _():
                remote(rp.at[n, k], rp.at[n, k], s2.at[n, k], q2.at[n, k], dev(x, y, z, other)).wait_recv()

            return 0

        lax.fori_loop(0, 16, go, 0)
        for h in (0, 1):
            v = rp[n, 8 * h].astype(F32)
            for k in range(1, 8):
                v = v + rp[n, 8 * h + k].astype(F32)
            out[0, :, h * HALF : (h + 1) * HALF] = v.astype(BF)

    loads[3].wait()
    first(
        0,
        lambda: dot(hid[...], wd[:, pl.ds(lo, HALF)], 1, 0),
        lambda: dot(hid[...], wd[:, pl.ds(hi, HALF)], 1, 0),
    )
    first_done(0)

    def stage3(mine, theirs):
        for d in (1, 3, 2):
            ring_copy(mine, d).wait_recv()
            core_copy(mine, d).start()

    per_core(stage3)
    second(0)

    def stage4(mine, theirs):
        for d in range(4):
            s = theirs(0)
            remote(s, s, s4.at[d], q4.at[d], dev(x, y, z, other)).wait_recv()

    per_core(stage4)

    hg = dot(cotg[...].reshape(256, 4096), wd[...], 1, 1)
    pg[...] = (hg * slope[...]).astype(BF)
    first(
        1,
        lambda: dot(pg[...], wu[pl.ds(lo, HALF), :], 1, 1),
        lambda: dot(pg[...], wu[pl.ds(hi, HALF), :], 1, 1),
    )
    first_done(1)
    second(1)

    outs = [
        pltpu.make_async_copy(cotg, cot_out, osem.at[0]),
        pltpu.make_async_copy(hid, hid_out, osem.at[1]),
        pltpu.make_async_copy(pg, pg_out, osem.at[2]),
    ]
    for o in outs:
        o.start()
    swap.wait_recv()
    prow_ref[...] = peer_msg[...].astype(F32)

    second_done(0)
    third(0)
    second_done(1)
    third(1)
    third_done(0, bo_ref)
    third_done(1, ig_ref)

    for o in outs:
        o.wait()
    swap.wait_send()

    def sent1(k, _):
        @pl.when(not_self0(k))
        def _():
            to_core0(k).wait_send()

        @pl.when(not_self1(k))
        def _():
            to_core1(k).wait_send()

        return 0

    lax.fori_loop(0, 8, sent1, 0)

    def sent2(mine, theirs):
        for d in (1, 2, 3):
            ring_copy(mine, d).wait_send()
        for d in range(4):
            core_copy(mine, d).wait_send()

    per_core(sent2)
    for n in (0, 1):
        remote(sb.at[n], rb.at[n], s0.at[n], q0.at[n], dev(x, y, z, other)).wait_send()
        for core in (0, 1):
            @pl.when(c == core)
            def _():
                for d in (1, 2, 3):
                    second_copy(n, d, core).wait_send()

        def sent3(k, _):
            @pl.when(k != plane * 4 + z * 2 + c)
            def _():
                third_copy(n, k).wait_send()

            return 0

        lax.fori_loop(0, 16, sent3, 0)


def step_call(x, cot, wu, wd, lp, plan, frag):
    hbm = pl.BlockSpec(memory_space=pl.ANY)
    smem = pl.BlockSpec(memory_space=pltpu.SMEM)
    vmem = pl.BlockSpec(memory_space=pltpu.VMEM)
    dma = pltpu.SemaphoreType.DMA
    return pl.pallas_call(
        step_kernel,
        out_shape=(
            jax.ShapeDtypeStruct((1, 4, 4096), BF),
            jax.ShapeDtypeStruct((1, 4, 4096), BF),
            jax.ShapeDtypeStruct((4, 4, 16, 4096), BF),
            jax.ShapeDtypeStruct((256, 512), BF),
            jax.ShapeDtypeStruct((256, 512), BF),
            jax.ShapeDtypeStruct((2, 16384), F32),
        ),
        in_specs=[hbm, hbm, hbm, hbm, hbm, smem, smem],
        out_specs=(vmem, vmem, hbm, hbm, hbm, vmem),
        scratch_shapes=[
            pltpu.VMEM((256, 4096), BF),
            pltpu.VMEM((4096, 512), BF),
            pltpu.VMEM((512, 4096), BF),
            pltpu.VMEM((16, 16384), F32),
            pltpu.VMEM((4, 4096), BF),
            pltpu.VMEM((16, 4, HALF), BF),
            pltpu.VMEM((4, 4, 16, 4096), BF),
            pltpu.VMEM((256, 512), F32),
            pltpu.VMEM((256, 512), BF),
            pltpu.VMEM((256, 512), BF),
            pltpu.VMEM((2, 16384), BF),
            pltpu.VMEM((2, 16384), BF),
            pltpu.VMEM((256, HALF), F32),
            pltpu.VMEM((2, 4, 4, 16, HALF), BF),
            pltpu.VMEM((2, 4, 4, 16, HALF), BF),
            pltpu.VMEM((2, 4, 4, 16, HALF), BF),
            pltpu.VMEM((2, 3, 4, 16, HALF), BF),
            pltpu.VMEM((2, 16, 4, HALF), BF),
            pltpu.VMEM((2, 16, 4, HALF), BF),
            dma((5,)), dma((3,)),
            dma((16,)), dma((16,)),
            dma((3,)), dma((3,)),
            dma((4,)), dma((4,)),
            dma((2,)), dma((2,)),
            dma((2, 3)), dma((2, 3)),
            dma((2, 16)), dma((2, 16)),
            dma((1,)), dma((1,)),
        ],
        compiler_params=pltpu.CompilerParams(collective_id=1, has_side_effects=True, vmem_limit_bytes=56 << 20),
        cost_estimate=pl.CostEstimate(flops=4 * 2 * 256 * 4096 * 512, bytes_accessed=14 << 20, transcendentals=1 << 17),
    )(x, cot, wu, wd, lp, plan, frag)


def update_kernel(
    plan_ref, frag_ref, bo_in, ig_in, x_ref, cot_ref, hid_ref, pg_ref, lp_ref, gp_ref, om_ref, prow_ref,
    bo_ref, ig_ref, ug_ref, dg_ref, ng_ref, nm_ref, ml_ref,
):
    @pl.when(pl.program_id(0) == 0)
    def _():
        bo_ref[...] = bo_in[...]
        ig_ref[...] = ig_in[...]

    dg_ref[0] = dot(hid_ref[...], cot_ref[...], 0, 0).astype(BF)
    ug_ref[0] = dot(x_ref[0], pg_ref[...], 0, 0).astype(BF)
    i0, i1 = selected_rows(plan_ref, frag_ref)
    mine, g, om = lp_ref[0], gp_ref[...], om_ref[...]
    row = lax.broadcasted_iota(jnp.int32, mine.shape, 0)
    keep = (row == i0) | (row == i1)
    peer = jnp.where(row == i0, prow_ref[0:1, :], prow_ref[1:2, :])
    delta = g - (mine.astype(BF).astype(F32) + peer) / 2
    momentum = 0.9 * om + delta
    updated = g - 0.7 * (delta + 0.9 * momentum)
    ng = jnp.where(keep, updated, g)
    nm_ref[...] = jnp.where(keep, momentum, om)
    ng_ref[...] = ng
    ml_ref[0] = jnp.where(keep, 0.5 * mine + 0.5 * ng, mine)


def update_call(plan, frag, bo, ig, x, cot, hid, pg, lp, gp, om, prow):
    steps = 4
    w, e = 4096 // steps, 16384 // steps
    smem = pl.BlockSpec(memory_space=pltpu.SMEM)
    whole3 = pl.BlockSpec((1, 4, 4096), lambda i: (0, 0, 0))
    act = pl.BlockSpec((256, 512), lambda i: (0, 0))
    params = pl.BlockSpec((16, e), lambda i: (0, i))
    params3 = pl.BlockSpec((1, 16, e), lambda i: (0, 0, i))
    return pl.pallas_call(
        update_kernel,
        grid=(steps,),
        out_shape=(
            jax.ShapeDtypeStruct((1, 4, 4096), BF),
            jax.ShapeDtypeStruct((1, 4, 4096), BF),
            jax.ShapeDtypeStruct((1, 4096, 512), BF),
            jax.ShapeDtypeStruct((1, 512, 4096), BF),
            jax.ShapeDtypeStruct((16, 16384), F32),
            jax.ShapeDtypeStruct((16, 16384), F32),
            jax.ShapeDtypeStruct((1, 16, 16384), F32),
        ),
        in_specs=[
            smem, smem, whole3, whole3,
            pl.BlockSpec((1, 256, w), lambda i: (0, 0, i)),
            pl.BlockSpec((256, w), lambda i: (0, i)),
            act, act, params3, params, params,
            pl.BlockSpec((2, e), lambda i: (0, i)),
        ],
        out_specs=(
            whole3, whole3,
            pl.BlockSpec((1, w, 512), lambda i: (0, i, 0)),
            pl.BlockSpec((1, 512, w), lambda i: (0, 0, i)),
            params, params, params3,
        ),
        compiler_params=pltpu.CompilerParams(vmem_limit_bytes=40 << 20),
        cost_estimate=pl.CostEstimate(flops=2 * 2 * 256 * 4096 * 512, bytes_accessed=18 << 20, transcendentals=0),
    )(plan, frag, bo, ig, x, cot, hid, pg, lp, gp, om, prow)


def on_device(inputs, cotangent, up_weight, down_weight, local_params, global_params, outer_momentum, plan, fragment_id):
    bo, ig, cot, hid, pg, prow = step_call(inputs, cotangent, up_weight, down_weight, local_params, plan, fragment_id)
    return update_call(
        plan, fragment_id, bo, ig, inputs, cot.reshape(256, 4096), hid, pg,
        local_params, global_params, outer_momentum, prow,
    )


def solution(mesh):
    placed = (
        P("replica", None, None),
        P("replica", "fsdp", None),
        P("replica", None, "fsdp"),
        P("replica", "fsdp", None),
        P("replica", None, "fsdp"),
        P(None, "fsdp"),
        P(None, "fsdp"),
        P(),
        P(),
    )
    return jax.shard_map(
        on_device,
        mesh=mesh,
        in_specs=placed,
        out_specs=(
            P("replica", "fsdp", None),
            P("replica", "fsdp", None),
            P("replica", None, "fsdp"),
            P("replica", "fsdp", None),
            P(None, "fsdp"),
            P(None, "fsdp"),
            P("replica", None, "fsdp"),
        ),
        check_vma=False,
    )
```

time: 491 us -> 59.1 us (0.12); the launches traced: 485 us -> 58.7 us
  blocking collectives: 322 us -> 0 us
  waiting for transfers between devices: 103 us -> 0 us
  Pallas kernels: 0 us -> 51.4 us
  matrix products: 27.4 us -> 0 us
  between operations: 16.9 us -> 1.38 us
  other arithmetic: 6.07 us -> 0 us
    unnamed x1 -> x0, blocking collectives: 322 us -> none
    all_gather x1 -> x0, waiting for transfers between devices: 70.8 us -> none  [on_device(): piece = lax.all_gather(grad_rows, 'fsdp', axis=0, tiled=True)]
    pallas_call x0 -> x2, Pallas kernels: none -> 51.4 us  [the longest x1 45.3 us: step_call(): pl.pallas_call(step_kernel, out_shape=(jax.ShapeDtypeStruct((1, 4, 4096),...]
    psum x1 -> x0, waiting for transfers between devices: 31.9 us -> none  [on_device(): total = lax.psum(mine.astype(jnp.bfloat16), 'replica').astype(jnp.float32)]
    dot_general x6 -> x0, matrix products: 27.4 us -> none  [the longest x2 10.5 us: contract_first(): lax.dot_general(left, right, (((0,), (0,)), ((), ())), preferred_element_...]
  transfers between devices with their start and end apart: 2 -> 0, of which waited for: 2 -> 0; matrix products, arithmetic and copies ran while one was open for 3% -> 0% of each run, Pallas kernels for 0% -> 0%
where the time goes in v1:
time: 59.1 us; the launch traced here: 58.7 us
  Pallas kernels  51.4 us (87%)
  local copies, waits for them, and re-layouts  5.92 us (10%)
  between operations  1.38 us (2%)
    pallas_call x1, Pallas kernels, step_call(): pl.pallas_call(step_kernel, out_shape=(jax.ShapeDtypeStruct((1, 4, 4096),...  45.3 us
    pallas_call x1, Pallas kernels, update_call(): pl.pallas_call(update_kernel, grid=(steps,), out_shape=(jax.ShapeDtypeStr...  6.05 us
    unnamed x22, local copies, waits for them, and re-layouts  5.92 us

profile of v1, /device:TPU:1, one launch (start us, length us, event | category | flops | bytes accessed | tf_op | source)
XLA Modules:
  0.0 58.7 jit_solution(304644101199414664)
XLA Ops:
  1.3 0.0 copy-start
  1.3 0.0 copy-start.2
  1.3 0.0 copy-start.3
  1.3 0.0 copy-start.4
  1.3 0.0 copy-start.10
  1.3 45.3 %shard_map.144 = (bf16[1,4,4096]{2,1,0:T(4,128)(2,1)}, bf16[1,4,4096]{2,1,0:T(4,128)(2,1)}, bf16[4,4,16,4096]{3,2,1,0:T(8,128)(2,1)}, bf16[256,512]{1,0:T(8,128)...) custom-call(bf16[1,256,4096]{2,1,0:T(8,128)(2,1)} %x_ref.1, bf16[1,4,4096]{2,1,0:T(4,128)(2,1)} %cot_hbm.1, ...), custom_call_target="tpu_custom_call" | custom-call | flops 4294967296 | bytes 14680064 | tf_op jit(solution)/shard_map/pallas_call | solution.py:339
  46.7 0.0 copy-done
  46.7 0.0 copy-done.2
  46.7 0.0 copy-done.3
  46.7 0.0 copy-done.4
  46.7 0.0 copy-done.10
  46.7 0.0 copy-start.1
  46.7 1.6 %copy-done.1 = bf16[4,4,16,4096]{3,2,1,0:T(8,128)(2,1)S(1)} copy-done((bf16[4,4,16,4096]{3,2,1,0:T(8,128)(2,1)S(1)}, bf16[4,4,16,4096]{3,2,1,0:T(8,128)(2,1)}, u32[]{:S(2)}) %copy-start.1) | copy-done | bytes 2097176
  48.3 0.0 copy-start.5
  48.3 0.9 %copy-done.5 = bf16[256,512]{1,0:T(8,128)(2,1)S(1)} copy-done((bf16[256,512]{1,0:T(8,128)(2,1)S(1)}, bf16[256,512]{1,0:T(8,128)(2,1)}, u32[]{:S(2)}) %copy-start.5) | copy-done | bytes 262168
  49.3 0.0 copy-start.6
  49.3 0.9 %copy-done.6 = bf16[256,512]{1,0:T(8,128)(2,1)S(1)} copy-done((bf16[256,512]{1,0:T(8,128)(2,1)S(1)}, bf16[256,512]{1,0:T(8,128)(2,1)}, u32[]{:S(2)}) %copy-start.6) | copy-done | bytes 262168
  50.2 0.0 copy-start.7
  50.2 0.9 %copy-done.7 = f32[2,16384]{1,0:T(2,128)S(1)} copy-done((f32[2,16384]{1,0:T(2,128)S(1)}, f32[2,16384]{1,0:T(2,128)}, u32[]{:S(2)}) %copy-start.7) | copy-done | bytes 131096
  51.1 0.0 copy-start.8
  51.1 0.8 %copy-done.8 = bf16[1,4,4096]{2,1,0:T(4,128)(2,1)S(1)} copy-done((bf16[1,4,4096]{2,1,0:T(4,128)(2,1)S(1)}, bf16[1,4,4096]{2,1,0:T(4,128)(2,1)}, u32[]{:S(2)}) %copy-start.8) | copy-done | bytes 32792
  51.9 0.0 copy-start.9
  51.9 0.8 %copy-done.9 = bf16[1,4,4096]{2,1,0:T(4,128)(2,1)S(1)} copy-done((bf16[1,4,4096]{2,1,0:T(4,128)(2,1)S(1)}, bf16[1,4,4096]{2,1,0:T(4,128)(2,1)}, u32[]{:S(2)}) %copy-start.9) | copy-done | bytes 32792
  52.6 6.1 %shard_map.145 = (bf16[1,4,4096]{2,1,0:T(4,128)(2,1)}, bf16[1,4,4096]{2,1,0:T(4,128)(2,1)}, bf16[1,4096,512]{2,1,0:T(8,128)(2,1)}, bf16[1,512,4096]{2,1,0:T(8,12...) custom-call(s32[16]{0:T(128)S(1)} %copy-done.10, s32[1]{0:T(128)S(6)} %copy.16.frag_ref, ...), custom_call_target="tpu_custom_call" | custom-call | flops 2147483648 | bytes 18874368 | tf_op jit(solution)/shard_map/pallas_call | solution.py:418
Async XLA Ops:
  1.3 45.4 %copy-start = (bf16[1,256,4096]{2,1,0:T(8,128)(2,1)S(1)}, bf16[1,256,4096]{2,1,0:T(8,128)(2,1)}, u32[]{:S(2)}) copy-start(bf16[1,256,4096]{2,1,0:T(8,128)(2,1)} %x_ref.1) | copy-start | bytes 6291460
  1.3 45.4 %copy-start.2 = (f32[1,16,16384]{2,1,0:T(8,128)S(1)}, f32[1,16,16384]{2,1,0:T(8,128)}, u32[]{:S(2)}) copy-start(f32[1,16,16384]{2,1,0:T(8,128)} %lp_ref.1) | copy-start | bytes 3145732
  1.3 45.4 %copy-start.3 = (f32[16,16384]{1,0:T(8,128)S(1)}, f32[16,16384]{1,0:T(8,128)}, u32[]{:S(2)}) copy-start(f32[16,16384]{1,0:T(8,128)} %gp_ref.1) | copy-start | bytes 3145732
  1.3 45.4 %copy-start.4 = (f32[16,16384]{1,0:T(8,128)S(1)}, f32[16,16384]{1,0:T(8,128)}, u32[]{:S(2)}) copy-start(f32[16,16384]{1,0:T(8,128)} %om_ref.1) | copy-start | bytes 3145732
  1.3 45.4 %copy-start.10 = (s32[16]{0:T(128)S(1)}, s32[16]{0:T(128)}, u32[]{:S(2)}) copy-start(s32[16]{0:T(128)} %plan_ref.3) | copy-start | bytes 196
  46.7 1.6 %copy-start.1 = (bf16[4,4,16,4096]{3,2,1,0:T(8,128)(2,1)S(1)}, bf16[4,4,16,4096]{3,2,1,0:T(8,128)(2,1)}, u32[]{:S(2)}) copy-start(bf16[4,4,16,4096]{3,2,1,0:T(8,128)(2,1)} %get-tuple-element.15) | copy-start | bytes 6291460
  48.3 0.9 %copy-start.5 = (bf16[256,512]{1,0:T(8,128)(2,1)S(1)}, bf16[256,512]{1,0:T(8,128)(2,1)}, u32[]{:S(2)}) copy-start(bf16[256,512]{1,0:T(8,128)(2,1)} %get-tuple-element.16.hid_ref) | copy-start | bytes 786436
  49.3 0.9 %copy-start.6 = (bf16[256,512]{1,0:T(8,128)(2,1)S(1)}, bf16[256,512]{1,0:T(8,128)(2,1)}, u32[]{:S(2)}) copy-start(bf16[256,512]{1,0:T(8,128)(2,1)} %get-tuple-element.17.pg_ref) | copy-start | bytes 786436
  50.2 0.9 %copy-start.7 = (f32[2,16384]{1,0:T(2,128)S(1)}, f32[2,16384]{1,0:T(2,128)}, u32[]{:S(2)}) copy-start(f32[2,16384]{1,0:T(2,128)} %get-tuple-element.18.prow_ref) | copy-start | bytes 393220
  51.1 0.8 %copy-start.8 = (bf16[1,4,4096]{2,1,0:T(4,128)(2,1)S(1)}, bf16[1,4,4096]{2,1,0:T(4,128)(2,1)}, u32[]{:S(2)}) copy-start(bf16[1,4,4096]{2,1,0:T(4,128)(2,1)} %get-tuple-element.13.bo_in) | copy-start | bytes 98308
  51.9 0.8 %copy-start.9 = (bf16[1,4,4096]{2,1,0:T(4,128)(2,1)S(1)}, bf16[1,4,4096]{2,1,0:T(4,128)(2,1)}, u32[]{:S(2)}) copy-start(bf16[1,4,4096]{2,1,0:T(4,128)(2,1)} %get-tuple-element.14.ig_in) | copy-start | bytes 98308

commit v2 on v1

--- a/solution.py
+++ b/solution.py
@@ -25,11 +25,11 @@
 
 
 def step_kernel(
-    x_hbm, cot_hbm, wu_hbm, wd_hbm, lp_hbm, plan_ref, frag_ref,
-    bo_ref, ig_ref, cot_out, hid_out, pg_out, prow_ref,
-    x_v, wu, wd, lp, cot4, st, cotg, slope, hid, pg, msg, peer_msg,
+    x_hbm, cot_hbm, wu_hbm, wd_hbm, lp_hbm, gp_hbm, om_hbm, plan_ref, frag_ref,
+    bo_ref, ig_ref, ug_ref, dg_ref, ng_ref, nm_ref, ml_ref,
+    x_v, wu, wd, lp, gp, om, cot4, st, cotg, slope, hid, pg, msg, peer_msg,
     own, sb, rb, part, r1, sp, rp,
-    lsem, osem, s1, q1, s3, q3, s4, q4, s0, q0, sr, qr, s2, q2, sx, qx,
+    lsem, s1, q1, s3, q3, s4, q4, s0, q0, sr, qr, s2, q2, sx, qx,
 ):
     rep = lax.axis_index("replica")
     f = lax.axis_index("fsdp")
@@ -51,34 +51,35 @@
             src_ref=src, dst_ref=dst, send_sem=ssem, recv_sem=rsem, device_id=device, device_id_type=MESH
         )
 
+    barrier = pltpu.get_barrier_semaphore()
+
+    def greet(k, _):
+        q, zz, cc = k // 4, (k // 2) % 2, k % 2
+
+        @pl.when(k != plane * 4 + z * 2 + c)
+        def _():
+            target = (rep, jnp.where(c == 0, x * 16 + q * 4, q * 16 + y * 4) + zz * 2 + cc)
+            pl.semaphore_signal(barrier, inc=1, device_id=target, device_id_type=MESH)
+
+        return 0
+
+    lax.fori_loop(0, 16, greet, 0)
+    for d in (1, 2, 3):
+        pl.semaphore_signal(barrier, inc=1, device_id=on_ring((ring + d) % 4), device_id_type=MESH)
+    pl.semaphore_signal(barrier, inc=1, device_id=(1 - rep, f), device_id_type=MESH)
+
     loads = [
         pltpu.make_async_copy(cot_hbm.at[0], cot4, lsem.at[0]),
         pltpu.make_async_copy(x_hbm.at[0], x_v, lsem.at[1]),
         pltpu.make_async_copy(wu_hbm.at[0], wu, lsem.at[2]),
         pltpu.make_async_copy(wd_hbm.at[0], wd, lsem.at[3]),
         pltpu.make_async_copy(lp_hbm.at[0], lp, lsem.at[4]),
+        pltpu.make_async_copy(gp_hbm, gp, lsem.at[5]),
+        pltpu.make_async_copy(om_hbm, om, lsem.at[6]),
     ]
-    for load in loads:
-        load.start()
-
-    barrier = pltpu.get_barrier_semaphore()
-
-    def greet(k, _):
-        u, zz, cc = k // 4, (k // 2) % 2, k % 2
-
-        @pl.when((u * 16 + y * 4 + zz * 2 + cc) != f)
-        def _():
-            pl.semaphore_signal(barrier, inc=1, device_id=dev(u, y, zz, cc), device_id_type=MESH)
-
-        @pl.when(u != y)
-        def _():
-            pl.semaphore_signal(barrier, inc=1, device_id=dev(x, u, zz, cc), device_id_type=MESH)
-
-        return 0
-
-    lax.fori_loop(0, 16, greet, 0)
-    pl.semaphore_signal(barrier, inc=1, device_id=(1 - rep, f), device_id_type=MESH)
-    pl.semaphore_wait(barrier, 28)
+    for k in (0, 1, 2, 4, 3, 5, 6):
+        loads[k].start()
+    pl.semaphore_wait(barrier, 19)
 
     loads[0].wait()
     st[plane * 4 + z * 2 + c] = cot4[:, pl.ds(lo, HALF)]
@@ -272,25 +273,34 @@
     first_done(1)
     second(1)
 
-    outs = [
-        pltpu.make_async_copy(cotg, cot_out, osem.at[0]),
-        pltpu.make_async_copy(hid, hid_out, osem.at[1]),
-        pltpu.make_async_copy(pg, pg_out, osem.at[2]),
-    ]
-    for o in outs:
-        o.start()
-    swap.wait_recv()
-    prow_ref[...] = peer_msg[...].astype(F32)
-
     second_done(0)
     third(0)
+
+    cot = cotg[...].reshape(256, 4096)
+    dg_ref[0] = dot(hid[...], cot, 0, 0).astype(BF)
+    ug_ref[0] = dot(x_v[...], pg[...], 0, 0).astype(BF)
+    loads[5].wait()
+    loads[6].wait()
+    swap.wait_recv()
+    for e in range(0, 16384, 2048):
+        cols = slice(e, e + 2048)
+        mine, g, mom = lp[:, cols], gp[:, cols], om[:, cols]
+        row = lax.broadcasted_iota(jnp.int32, mine.shape, 0)
+        keep = (row == i0) | (row == i1)
+        theirs = peer_msg[:, cols].astype(F32)
+        peer = jnp.where(row == i0, theirs[0:1, :], theirs[1:2, :])
+        delta = g - (mine.astype(BF).astype(F32) + peer) / 2
+        momentum = 0.9 * mom + delta
+        ng = jnp.where(keep, g - 0.7 * (delta + 0.9 * momentum), g)
+        nm_ref[:, cols] = jnp.where(keep, momentum, mom)
+        ng_ref[:, cols] = ng
+        ml_ref[0, :, cols] = jnp.where(keep, 0.5 * mine + 0.5 * ng, mine)
+
+    third_done(0, bo_ref)
     second_done(1)
     third(1)
-    third_done(0, bo_ref)
     third_done(1, ig_ref)
 
-    for o in outs:
-        o.wait()
     swap.wait_send()
 
     def sent1(k, _):
@@ -331,7 +341,7 @@
         lax.fori_loop(0, 16, sent3, 0)
 
 
-def step_call(x, cot, wu, wd, lp, plan, frag):
+def step_call(x, cot, wu, wd, lp, gp, om, plan, frag):
     hbm = pl.BlockSpec(memory_space=pl.ANY)
     smem = pl.BlockSpec(memory_space=pltpu.SMEM)
     vmem = pl.BlockSpec(memory_space=pltpu.VMEM)
@@ -339,19 +349,22 @@
     return pl.pallas_call(
         step_kernel,
         out_shape=(
-            jax.ShapeDtypeStruct((1, 4, 4096), BF),
-            jax.ShapeDtypeStruct((1, 4, 4096), BF),
-            jax.ShapeDtypeStruct((4, 4, 16, 4096), BF),
-            jax.ShapeDtypeStruct((256, 512), BF),
-            jax.ShapeDtypeStruct((256, 512), BF),
-            jax.ShapeDtypeStruct((2, 16384), F32),
+            pltpu.VMEM((1, 4, 4096), BF),
+            pltpu.VMEM((1, 4, 4096), BF),
+            pltpu.VMEM((1, 4096, 512), BF),
+            pltpu.VMEM((1, 512, 4096), BF),
+            pltpu.VMEM((16, 16384), F32),
+            pltpu.VMEM((16, 16384), F32),
+            pltpu.VMEM((1, 16, 16384), F32),
         ),
-        in_specs=[hbm, hbm, hbm, hbm, hbm, smem, smem],
-        out_specs=(vmem, vmem, hbm, hbm, hbm, vmem),
+        in_specs=[hbm] * 7 + [smem, smem],
+        out_specs=(vmem,) * 7,
         scratch_shapes=[
             pltpu.VMEM((256, 4096), BF),
             pltpu.VMEM((4096, 512), BF),
             pltpu.VMEM((512, 4096), BF),
+            pltpu.VMEM((16, 16384), F32),
+            pltpu.VMEM((16, 16384), F32),
             pltpu.VMEM((16, 16384), F32),
             pltpu.VMEM((4, 4096), BF),
             pltpu.VMEM((16, 4, HALF), BF),
@@ -368,7 +381,7 @@
             pltpu.VMEM((2, 3, 4, 16, HALF), BF),
             pltpu.VMEM((2, 16, 4, HALF), BF),
             pltpu.VMEM((2, 16, 4, HALF), BF),
-            dma((5,)), dma((3,)),
+            dma((7,)),
             dma((16,)), dma((16,)),
             dma((3,)), dma((3,)),
             dma((4,)), dma((4,)),
@@ -377,79 +390,38 @@
             dma((2, 16)), dma((2, 16)),
             dma((1,)), dma((1,)),
         ],
-        compiler_params=pltpu.CompilerParams(collective_id=1, has_side_effects=True, vmem_limit_bytes=56 << 20),
-        cost_estimate=pl.CostEstimate(flops=4 * 2 * 256 * 4096 * 512, bytes_accessed=14 << 20, transcendentals=1 << 17),
-    )(x, cot, wu, wd, lp, plan, frag)
-
-
-def update_kernel(
-    plan_ref, frag_ref, bo_in, ig_in, x_ref, cot_ref, hid_ref, pg_ref, lp_ref, gp_ref, om_ref, prow_ref,
-    bo_ref, ig_ref, ug_ref, dg_ref, ng_ref, nm_ref, ml_ref,
-):
-    @pl.when(pl.program_id(0) == 0)
-    def _():
-        bo_ref[...] = bo_in[...]
-        ig_ref[...] = ig_in[...]
-
-    dg_ref[0] = dot(hid_ref[...], cot_ref[...], 0, 0).astype(BF)
-    ug_ref[0] = dot(x_ref[0], pg_ref[...], 0, 0).astype(BF)
-    i0, i1 = selected_rows(plan_ref, frag_ref)
-    mine, g, om = lp_ref[0], gp_ref[...], om_ref[...]
-    row = lax.broadcasted_iota(jnp.int32, mine.shape, 0)
-    keep = (row == i0) | (row == i1)
-    peer = jnp.where(row == i0, prow_ref[0:1, :], prow_ref[1:2, :])
-    delta = g - (mine.astype(BF).astype(F32) + peer) / 2
-    momentum = 0.9 * om + delta
-    updated = g - 0.7 * (delta + 0.9 * momentum)
-    ng = jnp.where(keep, updated, g)
-    nm_ref[...] = jnp.where(keep, momentum, om)
-    ng_ref[...] = ng
-    ml_ref[0] = jnp.where(keep, 0.5 * mine + 0.5 * ng, mine)
-
-
-def update_call(plan, frag, bo, ig, x, cot, hid, pg, lp, gp, om, prow):
-    steps = 4
-    w, e = 4096 // steps, 16384 // steps
-    smem = pl.BlockSpec(memory_space=pltpu.SMEM)
-    whole3 = pl.BlockSpec((1, 4, 4096), lambda i: (0, 0, 0))
-    act = pl.BlockSpec((256, 512), lambda i: (0, 0))
-    params = pl.BlockSpec((16, e), lambda i: (0, i))
-    params3 = pl.BlockSpec((1, 16, e), lambda i: (0, 0, i))
+        compiler_params=pltpu.CompilerParams(collective_id=1, has_side_effects=True, vmem_limit_bytes=46 << 20),
+        cost_estimate=pl.CostEstimate(flops=6 * 2 * 256 * 4096 * 512, bytes_accessed=14 << 20, transcendentals=1 << 17),
+    )(x, cot, wu, wd, lp, gp, om, plan, frag)
+
+
+def write_kernel(*refs):
+    n = len(refs) // 2
+    copies = [pltpu.make_async_copy(refs[i], refs[n + i], refs[2 * n].at[i]) for i in range(n)]
+    for copy in copies:
+        copy.start()
+    for copy in copies:
+        copy.wait()
+
+
+def write_call(*arrays):
+    n = len(arrays)
     return pl.pallas_call(
-        update_kernel,
-        grid=(steps,),
-        out_shape=(
-            jax.ShapeDtypeStruct((1, 4, 4096), BF),
-            jax.ShapeDtypeStruct((1, 4, 4096), BF),
-            jax.ShapeDtypeStruct((1, 4096, 512), BF),
-            jax.ShapeDtypeStruct((1, 512, 4096), BF),
-            jax.ShapeDtypeStruct((16, 16384), F32),
-            jax.ShapeDtypeStruct((16, 16384), F32),
-            jax.ShapeDtypeStruct((1, 16, 16384), F32),
-        ),
-        in_specs=[
-            smem, smem, whole3, whole3,
-            pl.BlockSpec((1, 256, w), lambda i: (0, 0, i)),
-            pl.BlockSpec((256, w), lambda i: (0, i)),
-            act, act, params3, params, params,
-            pl.BlockSpec((2, e), lambda i: (0, i)),
-        ],
-        out_specs=(
-            whole3, whole3,
-            pl.BlockSpec((1, w, 512), lambda i: (0, i, 0)),
-            pl.BlockSpec((1, 512, w), lambda i: (0, 0, i)),
-            params, params, params3,
-        ),
-        compiler_params=pltpu.CompilerParams(vmem_limit_bytes=40 << 20),
-        cost_estimate=pl.CostEstimate(flops=2 * 2 * 256 * 4096 * 512, bytes_accessed=18 << 20, transcendentals=0),
-    )(plan, frag, bo, ig, x, cot, hid, pg, lp, gp, om, prow)
+        write_kernel,
+        out_shape=tuple(jax.ShapeDtypeStruct(a.shape, a.dtype) for a in arrays),
+        in_specs=[pl.BlockSpec(memory_space=pltpu.VMEM)] * n,
+        out_specs=tuple(pl.BlockSpec(memory_space=pl.ANY) for _ in arrays),
+        scratch_shapes=[pltpu.SemaphoreType.DMA((n,))],
+        compiler_params=pltpu.CompilerParams(has_side_effects=True, vmem_limit_bytes=16 << 20),
+        cost_estimate=pl.CostEstimate(flops=0, bytes_accessed=12 << 20, transcendentals=0),
+    )(*arrays)
 
 
 def on_device(inputs, cotangent, up_weight, down_weight, local_params, global_params, outer_momentum, plan, fragment_id):
-    bo, ig, cot, hid, pg, prow = step_call(inputs, cotangent, up_weight, down_weight, local_params, plan, fragment_id)
-    return update_call(
-        plan, fragment_id, bo, ig, inputs, cot.reshape(256, 4096), hid, pg,
-        local_params, global_params, outer_momentum, prow,
+    return write_call(
+        *step_call(
+            inputs, cotangent, up_weight, down_weight, local_params, global_params, outer_momentum, plan, fragment_id
+        )
     )
 
 

time: 59.1 us -> 50.1 us (0.85)
  local copies, waits for them, and re-layouts: 5.92 us -> 0 us
  Pallas kernels: 51.4 us -> 48.7 us
    unnamed x22 -> x0, local copies, waits for them, and re-layouts: 5.92 us -> none
    pallas_call x2, Pallas kernels: 51.4 us -> 48.7 us  [the longest x1 44.3 us: step_call(): pl.pallas_call(step_kernel, out_shape=(pltpu.VMEM((1, 4, 4096), BF), pltp...]
where the time goes in v2:
time: 50.1 us; the launch traced here: 50 us
  Pallas kernels  48.7 us (97%)
  between operations  1.29 us (3%)
    pallas_call x1, Pallas kernels, step_call(): pl.pallas_call(step_kernel, out_shape=(pltpu.VMEM((1, 4, 4096), BF), pltp...  44.3 us
    pallas_call x1, Pallas kernels, write_call(): pl.pallas_call(write_kernel, out_shape=tuple((jax.ShapeDtypeStruct(a.shap...  4.33 us

profile of v2, /device:TPU:1, one launch (start us, length us, event | category | flops | bytes accessed | tf_op | source)
XLA Modules:
  0.0 50.0 jit_solution(13185054795800992960)
XLA Ops:
  1.3 44.3 %shard_map.144 = (bf16[1,4,4096]{2,1,0:T(4,128)(2,1)S(1)}, bf16[1,4,4096]{2,1,0:T(4,128)(2,1)S(1)}, bf16[1,4096,512]{2,1,0:T(8,128)(2,1)S(1)}, bf16[1,512,4096]{...) custom-call(bf16[1,256,4096]{2,1,0:T(8,128)(2,1)} %x_hbm.1, ...), custom_call_target="tpu_custom_call" | custom-call | flops 6442450944 | bytes 14680064 | tf_op jit(solution)/shard_map/pallas_call | solution.py:349
  45.6 4.3 %shard_map.145 = (bf16[1,4,4096]{2,1,0:T(4,128)(2,1)}, bf16[1,4,4096]{2,1,0:T(4,128)(2,1)}, bf16[1,4096,512]{2,1,0:T(8,128)(2,1)}, bf16[1,512,4096]{2,1,0:T(8,12...) custom-call(bf16[1,4,4096]{2,1,0:T(4,128)(2,1)S(1)} %get-tuple-element.14.refs_0_, ...), custom_call_target="tpu_custom_call" | custom-call | bytes 12582912 | tf_op jit(solution)/shard_map/pallas_call | solution.py:409

commit v3 on v2

v3 whole, which is shorter than its diff:
```python
import jax
import jax.numpy as jnp
from jax import lax
from jax.experimental import pallas as pl
from jax.experimental.pallas import tpu as pltpu
from jax.sharding import PartitionSpec as P

BF = jnp.bfloat16
F32 = jnp.float32
MESH = pl.DeviceIdType.MESH
HALF = 2048
NEAR = (0, 1, 3, 2)
FAR = (2, 1, 3, 0)
PARTS = 2


def dot(a, b, ca, cb):
    return lax.dot_general(a, b, (((ca,), (cb,)), ((), ())), preferred_element_type=F32)


def selected_rows(plan_ref, frag_ref):
    first, last = jnp.int32(15), jnp.int32(0)
    for layer in range(16):
        hit = plan_ref[layer] == frag_ref[0]
        first = jnp.minimum(first, jnp.where(hit, layer, 15))
        last = jnp.maximum(last, jnp.where(hit, layer, 0))
    return first, last


def step_kernel(
    x_hbm, cot_hbm, wu_hbm, wd_hbm, lp_hbm, gp_hbm, om_hbm, plan_ref, frag_ref,
    bo_ref, ig_ref, ug_ref, dg_ref, ng_ref, nm_ref, ml_ref,
    x_v, wu, wd, lp, gp, om, cot4, st, cotg, slope, hid, pg, msg, peer_msg,
    own, sb, rb, part, r1, sp, rp,
    lsem, s1, q1, s3, q3, s4, q4, s0, q0, sr, qr, s2, q2, sx, qx,
):
    rep = lax.axis_index("replica")
    f = lax.axis_index("fsdp")
    x, y, z, c = f // 16, (f // 4) % 4, (f // 2) % 2, f % 2
    other = 1 - c
    lo = pl.multiple_of(c * HALF, HALF)
    hi = pl.multiple_of(other * HALF, HALF)
    ring = jnp.where(c == 0, x, y)
    plane = jnp.where(c == 0, y, x)

    ring_step = jnp.where(c == 0, 16, 4)
    plane_step = jnp.where(c == 0, 4, 16)
    here = plane * 4 + z * 2 + c
    peer = (rep, f + other - c)

    def on_ring(r):
        return (rep, f + (r - ring) * ring_step)

    def in_plane(k):
        return (rep, ring * ring_step + (k // 4) * plane_step + k % 4)

    def block_of(e):
        return (plane + e) % 4

    def rotate(k, fn):
        lax.fori_loop(1, 16, lambda d, _: (fn((k + d) % 16), 0)[1], 0)

    def remote(src, dst, ssem, rsem, device):
        return pltpu.make_async_remote_copy(
            src_ref=src, dst_ref=dst, send_sem=ssem, recv_sem=rsem, device_id=device, device_id_type=MESH
        )

    barrier = pltpu.get_barrier_semaphore()

    rotate(here, lambda k: pl.semaphore_signal(barrier, inc=1, device_id=in_plane(k), device_id_type=MESH))
    for d in (1, 2, 3):
        pl.semaphore_signal(barrier, inc=1, device_id=on_ring((ring + d) % 4), device_id_type=MESH)
    pl.semaphore_signal(barrier, inc=1, device_id=(1 - rep, f), device_id_type=MESH)

    loads = [
        pltpu.make_async_copy(cot_hbm.at[0], cot4, lsem.at[0]),
        pltpu.make_async_copy(x_hbm.at[0], x_v, lsem.at[1]),
        pltpu.make_async_copy(wu_hbm.at[0], wu, lsem.at[2]),
        pltpu.make_async_copy(wd_hbm.at[0], wd, lsem.at[3]),
        pltpu.make_async_copy(lp_hbm.at[0], lp, lsem.at[4]),
        pltpu.make_async_copy(gp_hbm, gp, lsem.at[5]),
        pltpu.make_async_copy(om_hbm, om, lsem.at[6]),
    ]
    for k in (0, 1, 2, 4, 3, 5, 6):
        loads[k].start()
    pl.semaphore_wait(barrier, 19)

    loads[0].wait()
    st[here] = cot4[:, pl.ds(lo, HALF)]

    def same_core(d):
        k = (plane * 2 + z + d) % 8
        target = ring * ring_step + (k // 2) * plane_step + (k % 2) * 2 + c
        return remote(cot4.at[:, pl.ds(lo, HALF)], st.at[here], s1.at[0], q1.at[plane], (rep, target))

    def other_core(d):
        k = (ring * 2 + z + d) % 8
        target = (k // 2) * ring_step + plane * plane_step + (k % 2) * 2 + other
        return remote(cot4.at[:, pl.ds(hi, HALF)], st.at[ring * 4 + z * 2 + c], s1.at[0], q1.at[ring], (rep, target))

    for d in range(8):
        if d:
            same_core(d).start()
        other_core(d).start()

    loads[4].wait()
    i0, i1 = selected_rows(plan_ref, frag_ref)
    msg[0:1, :] = lp[pl.ds(i0, 1), :].astype(BF)
    msg[1:2, :] = lp[pl.ds(i1, 1), :].astype(BF)
    swap = remote(msg, peer_msg, sx.at[0], qx.at[0], (1 - rep, f))
    swap.start()

    loads[1].wait()
    loads[2].wait()
    slope[...] = dot(x_v[...], wu[...], 1, 0)
    u = slope[...]
    t = jnp.tanh(0.7978845608 * (u + 0.044715 * u * u * u))
    hid[...] = (0.5 * u * (1.0 + t)).astype(BF)
    slope[...] = 0.5 * (1.0 + t) + 0.5 * u * (1.0 - t * t) * 0.7978845608 * (1.0 + 3.0 * 0.044715 * u * u)

    def block0(r, q):
        return cotg.at[r, q, :, pl.ds(0, HALF)]

    def block1(r, q):
        return cotg.at[q, r, :, pl.ds(HALF, HALF)]

    def ring_copy(block, e, d):
        b = block(ring, block_of(e))
        return remote(b, b, s3.at[0], q3.at[e, d - 1], on_ring((ring + d) % 4))

    def core_copy(block, e, d):
        b = block((ring + 4 - d) % 4, block_of(e))
        return remote(b, b, s4.at[0], q4.at[0], peer)

    def per_core(fn):
        @pl.when(c == 0)
        def _():
            fn(block0)

        @pl.when(c == 1)
        def _():
            fn(block1)

    def pieces(e):
        n = 4 if e else 3
        return remote(st.at[pl.ds(0, n)], st.at[pl.ds(0, n)], s1.at[0], q1.at[block_of(e)], peer)

    for e in NEAR:
        pieces(e).wait_recv()
        q = block_of(e)
        block = jnp.concatenate([st[4 * q + i].astype(F32) for i in range(4)], axis=0).astype(BF)

        def stage2(where):
            if where is block0:
                cotg[x, q, :, 0:HALF] = block
            else:
                cotg[q, y, :, HALF:] = block
            for d in (1, 3, 2):
                ring_copy(where, e, d).start()
            core_copy(where, e, 0).start()

        per_core(stage2)

    def across(n, cols):
        j = cols.start // cols.size
        return remote(sb.at[n, :, :, :, cols], rb.at[n, :, :, :, cols], s0.at[n, j], q0.at[n, j], peer)

    def first(n, chunks, product):
        for cols in chunks:
            sb[n, :, :, :, cols] = product(hi, cols).astype(BF).reshape(4, 4, 16, cols.size)
            across(n, cols).start()
        for cols in chunks:
            own[:, cols] = product(lo, cols)

    def first_done(n, cols):
        across(n, cols).wait_recv()
        total = own[:, cols].reshape(4, 4, 16, cols.size) + rb[n, :, :, :, cols].astype(F32)
        part[n, :, :, :, cols] = total.astype(BF)

    def second(n):
        for core in (0, 1):
            @pl.when(c == core)
            def _():
                for e in FAR:
                    q = block_of(e)
                    for d in (1, 3, 2):
                        r = (ring + d) % 4
                        src = part.at[n, r, q] if core == 0 else part.at[n, q, r]
                        remote(src, r1.at[n, d - 1, q], sr.at[n], qr.at[n, e], on_ring(r)).start()

    def third(n):
        slot = c * 8 + plane * 2 + z
        for e in FAR:
            q = block_of(e)
            got = r1.at[n, :, q]
            remote(got, got, sr.at[n], qr.at[n, e], peer).wait_recv()
            mine = jnp.where(c == 0, part[n, x, q].astype(F32), part[n, q, y].astype(F32))
            v = mine + r1[n, 0, q].astype(F32) + r1[n, 1, q].astype(F32) + r1[n, 2, q].astype(F32)
            for i in range(4):
                sp[n, 4 * q + i] = v[4 * i : 4 * i + 4].astype(BF)
            for i in range(0 if e else 1, 4):
                k = 4 * q + (z * 2 + c + i) % 4
                remote(sp.at[n, k], rp.at[n, slot], s2.at[n], q2.at[n], in_plane(k)).start()
        rp[n, slot] = sp[n, here]

    def third_all(n):
        return remote(sp.at[n, pl.ds(0, 15)], rp.at[n, pl.ds(0, 15)], s2.at[n], q2.at[n], peer)

    def third_done(n, out):
        third_all(n).wait_recv()
        for h in (0, 1):
            v = rp[n, 8 * h].astype(F32)
            for k in range(1, 8):
                v = v + rp[n, 8 * h + k].astype(F32)
            out[0, :, h * HALF : (h + 1) * HALF] = v.astype(BF)

    chunks = [pl.ds(j * HALF // PARTS, HALF // PARTS) for j in range(PARTS)]

    loads[3].wait()
    first(0, chunks, lambda at, cols: dot(hid[...], wd[:, pl.ds(at + cols.start, cols.size)], 1, 0))
    for cols in chunks:
        first_done(0, cols)

    loads[5].wait()
    loads[6].wait()
    swap.wait_recv()
    for e in range(0, 16384, 2048):
        cols = slice(e, e + 2048)
        mine, g, mom = lp[:, cols], gp[:, cols], om[:, cols]
        row = lax.broadcasted_iota(jnp.int32, mine.shape, 0)
        keep = (row == i0) | (row == i1)
        theirs = peer_msg[:, cols].astype(F32)
        far = jnp.where(row == i0, theirs[0:1, :], theirs[1:2, :])
        delta = g - (mine.astype(BF).astype(F32) + far) / 2
        momentum = 0.9 * mom + delta
        ng = jnp.where(keep, g - 0.7 * (delta + 0.9 * momentum), g)
        nm_ref[:, cols] = jnp.where(keep, momentum, mom)
        ng_ref[:, cols] = ng
        ml_ref[0, :, cols] = jnp.where(keep, 0.5 * mine + 0.5 * ng, mine)

    def stage3(where):
        for e in NEAR:
            for d in (1, 3, 2):
                ring_copy(where, e, d).wait_recv()
                core_copy(where, e, d).start()

    per_core(stage3)
    second(0)
    theirs = cotg.at[:, :, :, pl.ds(hi, HALF)]
    remote(theirs, theirs, s4.at[0], q4.at[0], peer).wait_recv()

    hg = dot(cotg[...].reshape(256, 4096), wd[...], 1, 1)
    pg[...] = (hg * slope[...]).astype(BF)
    first(1, chunks, lambda at, cols: dot(pg[...], wu[pl.ds(at + cols.start, cols.size), :], 1, 1))
    for cols in chunks:
        first_done(1, cols)
    second(1)
    third(0)

    dg_ref[0] = dot(hid[...], cotg[...].reshape(256, 4096), 0, 0).astype(BF)
    ug_ref[0] = dot(x_v[...], pg[...], 0, 0).astype(BF)
    third(1)
    third_done(0, bo_ref)
    third_done(1, ig_ref)

    swap.wait_send()
    remote(st.at[pl.ds(0, 15)], st.at[pl.ds(0, 15)], s1.at[0], q1.at[0], peer).wait_send()
    half = cotg.at[:, :, :, pl.ds(0, HALF)]
    most = cotg.at[pl.ds(0, 3), :, :, pl.ds(0, HALF)]
    remote(most, most, s3.at[0], q3.at[0, 0], peer).wait_send()
    remote(half, half, s4.at[0], q4.at[0], peer).wait_send()
    for n in (0, 1):
        for cols in chunks:
            across(n, cols).wait_send()
        remote(r1.at[n], r1.at[n], sr.at[n], qr.at[n, 0], peer).wait_send()
        third_all(n).wait_send()


def step_call(x, cot, wu, wd, lp, gp, om, plan, frag):
    hbm = pl.BlockSpec(memory_space=pl.ANY)
    smem = pl.BlockSpec(memory_space=pltpu.SMEM)
    vmem = pl.BlockSpec(memory_space=pltpu.VMEM)
    dma = pltpu.SemaphoreType.DMA
    return pl.pallas_call(
        step_kernel,
        out_shape=(
            pltpu.VMEM((1, 4, 4096), BF),
            pltpu.VMEM((1, 4, 4096), BF),
            pltpu.VMEM((1, 4096, 512), BF),
            pltpu.VMEM((1, 512, 4096), BF),
            pltpu.VMEM((16, 16384), F32),
            pltpu.VMEM((16, 16384), F32),
            pltpu.VMEM((1, 16, 16384), F32),
        ),
        in_specs=[hbm] * 7 + [smem, smem],
        out_specs=(vmem,) * 7,
        scratch_shapes=[
            pltpu.VMEM((256, 4096), BF),
            pltpu.VMEM((4096, 512), BF),
            pltpu.VMEM((512, 4096), BF),
            pltpu.VMEM((16, 16384), F32),
            pltpu.VMEM((16, 16384), F32),
            pltpu.VMEM((16, 16384), F32),
            pltpu.VMEM((4, 4096), BF),
            pltpu.VMEM((16, 4, HALF), BF),
            pltpu.VMEM((4, 4, 16, 4096), BF),
            pltpu.VMEM((256, 512), F32),
            pltpu.VMEM((256, 512), BF),
            pltpu.VMEM((256, 512), BF),
            pltpu.VMEM((2, 16384), BF),
            pltpu.VMEM((2, 16384), BF),
            pltpu.VMEM((256, HALF), F32),
            pltpu.VMEM((2, 4, 4, 16, HALF), BF),
            pltpu.VMEM((2, 4, 4, 16, HALF), BF),
            pltpu.VMEM((2, 4, 4, 16, HALF), BF),
            pltpu.VMEM((2, 3, 4, 16, HALF), BF),
            pltpu.VMEM((2, 16, 4, HALF), BF),
            pltpu.VMEM((2, 16, 4, HALF), BF),
            dma((7,)),
            dma((1,)), dma((4,)),
            dma((1,)), dma((4, 3)),
            dma((1,)), dma((1,)),
            dma((2, PARTS)), dma((2, PARTS)),
            dma((2,)), dma((2, 4)),
            dma((2,)), dma((2,)),
            dma((1,)), dma((1,)),
        ],
        compiler_params=pltpu.CompilerParams(collective_id=1, has_side_effects=True, vmem_limit_bytes=46 << 20),
        cost_estimate=pl.CostEstimate(flops=6 * 2 * 256 * 4096 * 512, bytes_accessed=14 << 20, transcendentals=1 << 17),
    )(x, cot, wu, wd, lp, gp, om, plan, frag)


def write_kernel(*refs):
    n = len(refs) // 2
    copies = [pltpu.make_async_copy(refs[i], refs[n + i], refs[2 * n].at[i]) for i in range(n)]
    for copy in copies:
        copy.start()
    for copy in copies:
        copy.wait()


def write_call(*arrays):
    n = len(arrays)
    return pl.pallas_call(
        write_kernel,
        out_shape=tuple(jax.ShapeDtypeStruct(a.shape, a.dtype) for a in arrays),
        in_specs=[pl.BlockSpec(memory_space=pltpu.VMEM)] * n,
        out_specs=tuple(pl.BlockSpec(memory_space=pl.ANY) for _ in arrays),
        scratch_shapes=[pltpu.SemaphoreType.DMA((n,))],
        compiler_params=pltpu.CompilerParams(has_side_effects=True, vmem_limit_bytes=16 << 20),
        cost_estimate=pl.CostEstimate(flops=0, bytes_accessed=12 << 20, transcendentals=0),
    )(*arrays)


def on_device(inputs, cotangent, up_weight, down_weight, local_params, global_params, outer_momentum, plan, fragment_id):
    return write_call(
        *step_call(
            inputs, cotangent, up_weight, down_weight, local_params, global_params, outer_momentum, plan, fragment_id
        )
    )


def solution(mesh):
    placed = (
        P("replica", None, None),
        P("replica", "fsdp", None),
        P("replica", None, "fsdp"),
        P("replica", "fsdp", None),
        P("replica", None, "fsdp"),
        P(None, "fsdp"),
        P(None, "fsdp"),
        P(),
        P(),
    )
    return jax.shard_map(
        on_device,
        mesh=mesh,
        in_specs=placed,
        out_specs=(
            P("replica", "fsdp", None),
            P("replica", "fsdp", None),
            P("replica", None, "fsdp"),
            P("replica", "fsdp", None),
            P(None, "fsdp"),
            P(None, "fsdp"),
            P("replica", None, "fsdp"),
        ),
        check_vma=False,
    )
```

time: 50.1 us -> 46.5 us (0.928)
  Pallas kernels: 48.7 us -> 45.1 us
    pallas_call x1, Pallas kernels: 44.3 us -> 40.8 us  [step_call(): pl.pallas_call(step_kernel, out_shape=(pltpu.VMEM((1, 4, 4096), BF), pltp...]
where the time goes in v3:
time: 46.5 us; the launch traced here: 46.4 us
  Pallas kernels  45.1 us (97%)
  between operations  1.29 us (3%)
    pallas_call x1, Pallas kernels, step_call(): pl.pallas_call(step_kernel, out_shape=(pltpu.VMEM((1, 4, 4096), BF), pltp...  40.8 us
    pallas_call x1, Pallas kernels, write_call(): pl.pallas_call(write_kernel, out_shape=tuple((jax.ShapeDtypeStruct(a.shap...  4.33 us

profile of v3, /device:TPU:1, one launch (start us, length us, event | category | flops | bytes accessed | tf_op | source)
XLA Modules:
  0.0 46.4 jit_solution(1958199900388975465)
XLA Ops:
  1.3 40.8 %shard_map.144 = (bf16[1,4,4096]{2,1,0:T(4,128)(2,1)S(1)}, bf16[1,4,4096]{2,1,0:T(4,128)(2,1)S(1)}, bf16[1,4096,512]{2,1,0:T(8,128)(2,1)S(1)}, bf16[1,512,4096]{...) custom-call(bf16[1,256,4096]{2,1,0:T(8,128)(2,1)} %x_hbm.1, ...), custom_call_target="tpu_custom_call" | custom-call | flops 6442450944 | bytes 14680064 | tf_op jit(solution)/shard_map/pallas_call | solution.py:284
  42.1 4.3 %shard_map.145 = (bf16[1,4,4096]{2,1,0:T(4,128)(2,1)}, bf16[1,4,4096]{2,1,0:T(4,128)(2,1)}, bf16[1,4096,512]{2,1,0:T(8,128)(2,1)}, bf16[1,512,4096]{2,1,0:T(8,12...) custom-call(bf16[1,4,4096]{2,1,0:T(4,128)(2,1)S(1)} %get-tuple-element.14.refs_0_, ...), custom_call_target="tpu_custom_call" | custom-call | bytes 12582912 | tf_op jit(solution)/shard_map/pallas_call | solution.py:344

commit v4 on v3

--- a/solution.py
+++ b/solution.py
@@ -11,7 +11,6 @@
 HALF = 2048
 NEAR = (0, 1, 3, 2)
 FAR = (2, 1, 3, 0)
-PARTS = 2
 
 
 def dot(a, b, ca, cb):
@@ -28,9 +27,9 @@
 
 
 def step_kernel(
-    x_hbm, cot_hbm, wu_hbm, wd_hbm, lp_hbm, gp_hbm, om_hbm, plan_ref, frag_ref,
+    x_hbm, cot_hbm, wu_hbm, wd_hbm, lp_hbm, gp_hbm, om_hbm, plan_hbm, frag_hbm,
     bo_ref, ig_ref, ug_ref, dg_ref, ng_ref, nm_ref, ml_ref,
-    x_v, wu, wd, lp, gp, om, cot4, st, cotg, slope, hid, pg, msg, peer_msg,
+    plan_ref, frag_ref, x_v, wu, wd, lp, gp, om, cot4, st, cotg, slope, hg, hid, pg, msg, peer_msg,
     own, sb, rb, part, r1, sp, rp,
     lsem, s1, q1, s3, q3, s4, q4, s0, q0, sr, qr, s2, q2, sx, qx,
 ):
@@ -80,8 +79,10 @@
         pltpu.make_async_copy(lp_hbm.at[0], lp, lsem.at[4]),
         pltpu.make_async_copy(gp_hbm, gp, lsem.at[5]),
         pltpu.make_async_copy(om_hbm, om, lsem.at[6]),
+        pltpu.make_async_copy(plan_hbm, plan_ref, lsem.at[7]),
+        pltpu.make_async_copy(frag_hbm, frag_ref, lsem.at[8]),
     ]
-    for k in (0, 1, 2, 4, 3, 5, 6):
+    for k in (0, 7, 8, 1, 2, 4, 3, 5, 6):
         loads[k].start()
     pl.semaphore_wait(barrier, 19)
 
@@ -104,6 +105,8 @@
         other_core(d).start()
 
     loads[4].wait()
+    loads[7].wait()
+    loads[8].wait()
     i0, i1 = selected_rows(plan_ref, frag_ref)
     msg[0:1, :] = lp[pl.ds(i0, 1), :].astype(BF)
     msg[1:2, :] = lp[pl.ds(i1, 1), :].astype(BF)
@@ -161,32 +164,39 @@
 
         per_core(stage2)
 
-    def across(n, cols):
-        j = cols.start // cols.size
-        return remote(sb.at[n, :, :, :, cols], rb.at[n, :, :, :, cols], s0.at[n, j], q0.at[n, j], peer)
-
-    def first(n, chunks, product):
-        for cols in chunks:
-            sb[n, :, :, :, cols] = product(hi, cols).astype(BF).reshape(4, 4, 16, cols.size)
-            across(n, cols).start()
-        for cols in chunks:
-            own[:, cols] = product(lo, cols)
-
-    def first_done(n, cols):
-        across(n, cols).wait_recv()
-        total = own[:, cols].reshape(4, 4, 16, cols.size) + rb[n, :, :, :, cols].astype(F32)
-        part[n, :, :, :, cols] = total.astype(BF)
-
-    def second(n):
+    def first(n, product):
+        sb[n] = product(hi).astype(BF).reshape(4, 4, 16, HALF)
         for core in (0, 1):
             @pl.when(c == core)
             def _():
                 for e in FAR:
-                    q = block_of(e)
-                    for d in (1, 3, 2):
-                        r = (ring + d) % 4
-                        src = part.at[n, r, q] if core == 0 else part.at[n, q, r]
-                        remote(src, r1.at[n, d - 1, q], sr.at[n], qr.at[n, e], on_ring(r)).start()
+                    q = (ring + e) % 4
+                    src, dst = (sb.at[n, q], rb.at[n, q]) if core == 0 else (sb.at[n, :, q], rb.at[n, :, q])
+                    remote(src, dst, s0.at[n], q0.at[n, e], peer).start()
+        own[...] = product(lo).reshape(4, 4, 16, HALF)
+
+    def combine(n, core, e):
+        q = block_of(e)
+        remote(rb.at[n, 0], rb.at[n, 0], s0.at[n], q0.at[n, e], peer).wait_recv()
+        if core == 0:
+            part[n, :, q] = (own[:, q] + rb[n, :, q].astype(F32)).astype(BF)
+        else:
+            part[n, q] = (own[q] + rb[n, q].astype(F32)).astype(BF)
+
+    def ring_send(n, core, e):
+        q = block_of(e)
+        for d in (1, 3, 2):
+            r = (ring + d) % 4
+            src = part.at[n, r, q] if core == 0 else part.at[n, q, r]
+            remote(src, r1.at[n, d - 1, q], sr.at[n], qr.at[n, e], on_ring(r)).start()
+
+    def blocks(*acts):
+        for core in (0, 1):
+            @pl.when(c == core)
+            def _():
+                for e in FAR:
+                    for act in acts:
+                        act(core, e)
 
     def third(n):
         slot = c * 8 + plane * 2 + z
@@ -214,12 +224,9 @@
                 v = v + rp[n, 8 * h + k].astype(F32)
             out[0, :, h * HALF : (h + 1) * HALF] = v.astype(BF)
 
-    chunks = [pl.ds(j * HALF // PARTS, HALF // PARTS) for j in range(PARTS)]
-
     loads[3].wait()
-    first(0, chunks, lambda at, cols: dot(hid[...], wd[:, pl.ds(at + cols.start, cols.size)], 1, 0))
-    for cols in chunks:
-        first_done(0, cols)
+    first(0, lambda at: dot(hid[...], wd[:, pl.ds(at, HALF)], 1, 0))
+    blocks(lambda core, e: combine(0, core, e))
 
     loads[5].wait()
     loads[6].wait()
@@ -239,26 +246,32 @@
         ml_ref[0, :, cols] = jnp.where(keep, 0.5 * mine + 0.5 * ng, mine)
 
     def stage3(where):
-        for e in NEAR:
+        for i, e in enumerate(NEAR):
+            if i == 3:
+                most = cotg.at[pl.ds(0, 3), :, :, pl.ds(0, HALF)]
+                remote(most, most, s3.at[0], q3.at[0, 0], peer).wait_send()
+                for b in FAR:
+                    ring_send(0, 0 if where is block0 else 1, b)
             for d in (1, 3, 2):
                 ring_copy(where, e, d).wait_recv()
                 core_copy(where, e, d).start()
 
     per_core(stage3)
-    second(0)
+
+    def half_grad(at):
+        return dot(cotg[:, :, :, pl.ds(at, HALF)].reshape(256, HALF), wd[:, pl.ds(at, HALF)], 1, 1)
+
+    hg[...] = half_grad(lo)
     theirs = cotg.at[:, :, :, pl.ds(hi, HALF)]
     remote(theirs, theirs, s4.at[0], q4.at[0], peer).wait_recv()
 
-    hg = dot(cotg[...].reshape(256, 4096), wd[...], 1, 1)
-    pg[...] = (hg * slope[...]).astype(BF)
-    first(1, chunks, lambda at, cols: dot(pg[...], wu[pl.ds(at + cols.start, cols.size), :], 1, 1))
-    for cols in chunks:
-        first_done(1, cols)
-    second(1)
-    third(0)
+    pg[...] = ((hg[...] + half_grad(hi)) * slope[...]).astype(BF)
+    first(1, lambda at: dot(pg[...], wu[pl.ds(at, HALF), :], 1, 1))
+    blocks(lambda core, e: combine(1, core, e), lambda core, e: ring_send(1, core, e))
 
     dg_ref[0] = dot(hid[...], cotg[...].reshape(256, 4096), 0, 0).astype(BF)
     ug_ref[0] = dot(x_v[...], pg[...], 0, 0).astype(BF)
+    third(0)
     third(1)
     third_done(0, bo_ref)
     third_done(1, ig_ref)
@@ -266,12 +279,9 @@
     swap.wait_send()
     remote(st.at[pl.ds(0, 15)], st.at[pl.ds(0, 15)], s1.at[0], q1.at[0], peer).wait_send()
     half = cotg.at[:, :, :, pl.ds(0, HALF)]
-    most = cotg.at[pl.ds(0, 3), :, :, pl.ds(0, HALF)]
-    remote(most, most, s3.at[0], q3.at[0, 0], peer).wait_send()
     remote(half, half, s4.at[0], q4.at[0], peer).wait_send()
     for n in (0, 1):
-        for cols in chunks:
-            across(n, cols).wait_send()
+        remote(sb.at[n], rb.at[n], s0.at[n], q0.at[n, 0], peer).wait_send()
         remote(r1.at[n], r1.at[n], sr.at[n], qr.at[n, 0], peer).wait_send()
         third_all(n).wait_send()
 
@@ -292,9 +302,11 @@
             pltpu.VMEM((16, 16384), F32),
             pltpu.VMEM((1, 16, 16384), F32),
         ),
-        in_specs=[hbm] * 7 + [smem, smem],
+        in_specs=[hbm] * 9,
         out_specs=(vmem,) * 7,
         scratch_shapes=[
+            pltpu.SMEM((16,), jnp.int32),
+            pltpu.SMEM((1,), jnp.int32),
             pltpu.VMEM((256, 4096), BF),
             pltpu.VMEM((4096, 512), BF),
             pltpu.VMEM((512, 4096), BF),
@@ -305,22 +317,23 @@
             pltpu.VMEM((16, 4, HALF), BF),
             pltpu.VMEM((4, 4, 16, 4096), BF),
             pltpu.VMEM((256, 512), F32),
+            pltpu.VMEM((256, 512), F32),
             pltpu.VMEM((256, 512), BF),
             pltpu.VMEM((256, 512), BF),
             pltpu.VMEM((2, 16384), BF),
             pltpu.VMEM((2, 16384), BF),
-            pltpu.VMEM((256, HALF), F32),
+            pltpu.VMEM((4, 4, 16, HALF), F32),
             pltpu.VMEM((2, 4, 4, 16, HALF), BF),
             pltpu.VMEM((2, 4, 4, 16, HALF), BF),
             pltpu.VMEM((2, 4, 4, 16, HALF), BF),
             pltpu.VMEM((2, 3, 4, 16, HALF), BF),
             pltpu.VMEM((2, 16, 4, HALF), BF),
             pltpu.VMEM((2, 16, 4, HALF), BF),
-            dma((7,)),
+            dma((9,)),
             dma((1,)), dma((4,)),
             dma((1,)), dma((4, 3)),
             dma((1,)), dma((1,)),
-            dma((2, PARTS)), dma((2, PARTS)),
+            dma((2,)), dma((2, 4)),
             dma((2,)), dma((2, 4)),
             dma((2,)), dma((2,)),
             dma((1,)), dma((1,)),

time: 46.5 us -> 44.7 us (0.961)
  Pallas kernels: 45.1 us -> 43.3 us
    pallas_call x1, Pallas kernels: 40.8 us -> 38.9 us  [step_call(): pl.pallas_call(step_kernel, out_shape=(pltpu.VMEM((1, 4, 4096), BF), pltp...]
where the time goes in v4:
time: 44.7 us; the launch traced here: 44.6 us
  Pallas kernels  43.3 us (97%)
  between operations  1.29 us (3%)
    pallas_call x1, Pallas kernels, step_call(): pl.pallas_call(step_kernel, out_shape=(pltpu.VMEM((1, 4, 4096), BF), pltp...  38.9 us
    pallas_call x1, Pallas kernels, write_call(): pl.pallas_call(write_kernel, out_shape=tuple((jax.ShapeDtypeStruct(a.shap...  4.33 us

profile of v4, /device:TPU:1, one launch (start us, length us, event | category | flops | bytes accessed | tf_op | source)
XLA Modules:
  0.0 44.6 jit_solution(14970410740594495801)
XLA Ops:
  1.3 38.9 %shard_map.144 = (bf16[1,4,4096]{2,1,0:T(4,128)(2,1)S(1)}, bf16[1,4,4096]{2,1,0:T(4,128)(2,1)S(1)}, bf16[1,4096,512]{2,1,0:T(8,128)(2,1)S(1)}, bf16[1,512,4096]{...) custom-call(bf16[1,256,4096]{2,1,0:T(8,128)(2,1)} %x_hbm.1, ...), custom_call_target="tpu_custom_call" | custom-call | flops 6442450944 | bytes 14680064 | tf_op jit(solution)/shard_map/pallas_call | solution.py:294
  40.2 4.3 %shard_map.145 = (bf16[1,4,4096]{2,1,0:T(4,128)(2,1)}, bf16[1,4,4096]{2,1,0:T(4,128)(2,1)}, bf16[1,4096,512]{2,1,0:T(8,128)(2,1)}, bf16[1,512,4096]{2,1,0:T(8,12...) custom-call(bf16[1,4,4096]{2,1,0:T(4,128)(2,1)S(1)} %get-tuple-element.14.refs_0_, ...), custom_call_target="tpu_custom_call" | custom-call | bytes 12582912 | tf_op jit(solution)/shard_map/pallas_call | solution.py:357

commit v5 on v4

--- a/solution.py
+++ b/solution.py
@@ -82,7 +82,7 @@
         pltpu.make_async_copy(plan_hbm, plan_ref, lsem.at[7]),
         pltpu.make_async_copy(frag_hbm, frag_ref, lsem.at[8]),
     ]
-    for k in (0, 7, 8, 1, 2, 4, 3, 5, 6):
+    for k in (0, 1, 2, 3, 7, 8, 4, 5, 6):
         loads[k].start()
     pl.semaphore_wait(barrier, 19)
 
@@ -90,19 +90,68 @@
     st[here] = cot4[:, pl.ds(lo, HALF)]
 
     def same_core(d):
-        k = (plane * 2 + z + d) % 8
-        target = ring * ring_step + (k // 2) * plane_step + (k % 2) * 2 + c
+        target = ring * ring_step + block_of(NEAR[d // 2]) * plane_step + (z + d) % 2 * 2 + c
         return remote(cot4.at[:, pl.ds(lo, HALF)], st.at[here], s1.at[0], q1.at[plane], (rep, target))
 
     def other_core(d):
-        k = (ring * 2 + z + d) % 8
-        target = (k // 2) * ring_step + plane * plane_step + (k % 2) * 2 + other
+        target = (ring + NEAR[d // 2]) % 4 * ring_step + plane * plane_step + (z + d) % 2 * 2 + other
         return remote(cot4.at[:, pl.ds(hi, HALF)], st.at[ring * 4 + z * 2 + c], s1.at[0], q1.at[ring], (rep, target))
 
     for d in range(8):
         if d:
             same_core(d).start()
         other_core(d).start()
+
+    loads[1].wait()
+    loads[2].wait()
+    slope[...] = dot(x_v[...], wu[...], 1, 0)
+    u = slope[...]
+    t = jnp.tanh(0.7978845608 * (u + 0.044715 * u * u * u))
+    hid[...] = (0.5 * u * (1.0 + t)).astype(BF)
+    slope[...] = 0.5 * (1.0 + t) + 0.5 * u * (1.0 - t * t) * 0.7978845608 * (1.0 + 3.0 * 0.044715 * u * u)
+
+    def block0(r, q):
+        return cotg.at[r, q, :, pl.ds(0, HALF)]
+
+    def block1(r, q):
+        return cotg.at[q, r, :, pl.ds(HALF, HALF)]
+
+    def ring_copy(block, e, d):
+        b = block(ring, block_of(e))
+        return remote(b, b, s3.at[0], q3.at[e, d - 1], on_ring((ring + d) % 4))
+
+    def core_copy(block, e, d):
+        b = block((ring + 4 - d) % 4, block_of(e))
+        return remote(b, b, s4.at[0], q4.at[0], peer)
+
+    def per_core(fn):
+        @pl.when(c == 0)
+        def _():
+            fn(block0)
+
+        @pl.when(c == 1)
+        def _():
+            fn(block1)
+
+    def pieces(e):
+        n = 4 if e else 3
+        return remote(st.at[pl.ds(0, n)], st.at[pl.ds(0, n)], s1.at[0], q1.at[block_of(e)], peer)
+
+    for e in NEAR:
+        pieces(e).wait_recv()
+        q = block_of(e)
+        block = jnp.concatenate([st[4 * q + i].astype(F32) for i in range(4)], axis=0).astype(BF)
+
+        def stage2(where):
+            if where is block0:
+                cotg[x, q, :, 0:HALF] = block
+            else:
+                cotg[q, y, :, HALF:] = block
+            for d in (2, 1, 3):
+                ring_copy(where, e, d).start()
+            core_copy(where, e, 0).start()
+
+        per_core(stage2)
 
     loads[4].wait()
     loads[7].wait()
@@ -112,57 +161,6 @@
     msg[1:2, :] = lp[pl.ds(i1, 1), :].astype(BF)
     swap = remote(msg, peer_msg, sx.at[0], qx.at[0], (1 - rep, f))
     swap.start()
-
-    loads[1].wait()
-    loads[2].wait()
-    slope[...] = dot(x_v[...], wu[...], 1, 0)
-    u = slope[...]
-    t = jnp.tanh(0.7978845608 * (u + 0.044715 * u * u * u))
-    hid[...] = (0.5 * u * (1.0 + t)).astype(BF)
-    slope[...] = 0.5 * (1.0 + t) + 0.5 * u * (1.0 - t * t) * 0.7978845608 * (1.0 + 3.0 * 0.044715 * u * u)
-
-    def block0(r, q):
-        return cotg.at[r, q, :, pl.ds(0, HALF)]
-
-    def block1(r, q):
-        return cotg.at[q, r, :, pl.ds(HALF, HALF)]
-
-    def ring_copy(block, e, d):
-        b = block(ring, block_of(e))
-        return remote(b, b, s3.at[0], q3.at[e, d - 1], on_ring((ring + d) % 4))
-
-    def core_copy(block, e, d):
-        b = block((ring + 4 - d) % 4, block_of(e))
-        return remote(b, b, s4.at[0], q4.at[0], peer)
-
-    def per_core(fn):
-        @pl.when(c == 0)
-        def _():
-            fn(block0)
-
-        @pl.when(c == 1)
-        def _():
-            fn(block1)
-
-    def pieces(e):
-        n = 4 if e else 3
-        return remote(st.at[pl.ds(0, n)], st.at[pl.ds(0, n)], s1.at[0], q1.at[block_of(e)], peer)
-
-    for e in NEAR:
-        pieces(e).wait_recv()
-        q = block_of(e)
-        block = jnp.concatenate([st[4 * q + i].astype(F32) for i in range(4)], axis=0).astype(BF)
-
-        def stage2(where):
-            if where is block0:
-                cotg[x, q, :, 0:HALF] = block
-            else:
-                cotg[q, y, :, HALF:] = block
-            for d in (1, 3, 2):
-                ring_copy(where, e, d).start()
-            core_copy(where, e, 0).start()
-
-        per_core(stage2)
 
     def first(n, product):
         sb[n] = product(hi).astype(BF).reshape(4, 4, 16, HALF)
@@ -185,7 +183,7 @@
 
     def ring_send(n, core, e):
         q = block_of(e)
-        for d in (1, 3, 2):
+        for d in (2, 1, 3):
             r = (ring + d) % 4
             src = part.at[n, r, q] if core == 0 else part.at[n, q, r]
             remote(src, r1.at[n, d - 1, q], sr.at[n], qr.at[n, e], on_ring(r)).start()
@@ -208,7 +206,7 @@
             v = mine + r1[n, 0, q].astype(F32) + r1[n, 1, q].astype(F32) + r1[n, 2, q].astype(F32)
             for i in range(4):
                 sp[n, 4 * q + i] = v[4 * i : 4 * i + 4].astype(BF)
-            for i in range(0 if e else 1, 4):
+            for i in (2, 3, 0, 1) if e else (2, 3, 1):
                 k = 4 * q + (z * 2 + c + i) % 4
                 remote(sp.at[n, k], rp.at[n, slot], s2.at[n], q2.at[n], in_plane(k)).start()
         rp[n, slot] = sp[n, here]
@@ -227,6 +225,35 @@
     loads[3].wait()
     first(0, lambda at: dot(hid[...], wd[:, pl.ds(at, HALF)], 1, 0))
     blocks(lambda core, e: combine(0, core, e))
+
+    def stage3(where):
+        for i, e in enumerate(NEAR):
+            if i == 3:
+                most = cotg.at[pl.ds(0, 3), :, :, pl.ds(0, HALF)]
+                remote(most, most, s3.at[0], q3.at[0, 0], peer).wait_send()
+                for b in FAR:
+                    ring_send(0, 0 if where is block0 else 1, b)
+            for d in (2, 1, 3):
+                ring_copy(where, e, d).wait_recv()
+                core_copy(where, e, d).start()
+
+    per_core(stage3)
+
+    def half_grad(at):
+        return dot(cotg[:, :, :, pl.ds(at, HALF)].reshape(256, HALF), wd[:, pl.ds(at, HALF)], 1, 1)
+
+    hg[...] = half_grad(lo)
+    theirs = cotg.at[:, :, :, pl.ds(hi, HALF)]
+    remote(theirs, theirs, s4.at[0], q4.at[0], peer).wait_recv()
+
+    pg[...] = ((hg[...] + half_grad(hi)) * slope[...]).astype(BF)
+    first(1, lambda at: dot(pg[...], wu[pl.ds(at, HALF), :], 1, 1))
+    blocks(lambda core, e: combine(1, core, e), lambda core, e: ring_send(1, core, e))
+
+    dg_ref[0] = dot(hid[...], cotg[...].reshape(256, 4096), 0, 0).astype(BF)
+    ug_ref[0] = dot(x_v[...], pg[...], 0, 0).astype(BF)
+    third(0)
+    third(1)
 
     loads[5].wait()
     loads[6].wait()
@@ -245,34 +272,6 @@
         ng_ref[:, cols] = ng
         ml_ref[0, :, cols] = jnp.where(keep, 0.5 * mine + 0.5 * ng, mine)
 
-    def stage3(where):
-        for i, e in enumerate(NEAR):
-            if i == 3:
-                most = cotg.at[pl.ds(0, 3), :, :, pl.ds(0, HALF)]
-                remote(most, most, s3.at[0], q3.at[0, 0], peer).wait_send()
-                for b in FAR:
-                    ring_send(0, 0 if where is block0 else 1, b)
-            for d in (1, 3, 2):
-                ring_copy(where, e, d).wait_recv()
-                core_copy(where, e, d).start()
-
-    per_core(stage3)
-
-    def half_grad(at):
-        return dot(cotg[:, :, :, pl.ds(at, HALF)].reshape(256, HALF), wd[:, pl.ds(at, HALF)], 1, 1)
-
-    hg[...] = half_grad(lo)
-    theirs = cotg.at[:, :, :, pl.ds(hi, HALF)]
-    remote(theirs, theirs, s4.at[0], q4.at[0], peer).wait_recv()
-
-    pg[...] = ((hg[...] + half_grad(hi)) * slope[...]).astype(BF)
-    first(1, lambda at: dot(pg[...], wu[pl.ds(at, HALF), :], 1, 1))
-    blocks(lambda core, e: combine(1, core, e), lambda core, e: ring_send(1, core, e))
-
-    dg_ref[0] = dot(hid[...], cotg[...].reshape(256, 4096), 0, 0).astype(BF)
-    ug_ref[0] = dot(x_v[...], pg[...], 0, 0).astype(BF)
-    third(0)
-    third(1)
     third_done(0, bo_ref)
     third_done(1, ig_ref)
 

time: 44.7 us -> 43.6 us (0.975)
  Pallas kernels: 43.3 us -> 42.1 us
    pallas_call x1, Pallas kernels: 38.9 us -> 37.8 us  [step_call(): pl.pallas_call(step_kernel, out_shape=(pltpu.VMEM((1, 4, 4096), BF), pltp...]
where the time goes in v5:
time: 43.6 us; the launch traced here: 43.4 us
  Pallas kernels  42.1 us (97%)
  between operations  1.29 us (3%)
    pallas_call x1, Pallas kernels, step_call(): pl.pallas_call(step_kernel, out_shape=(pltpu.VMEM((1, 4, 4096), BF), pltp...  37.8 us
    pallas_call x1, Pallas kernels, write_call(): pl.pallas_call(write_kernel, out_shape=tuple((jax.ShapeDtypeStruct(a.shap...  4.33 us

profile of v5, /device:TPU:1, one launch (start us, length us, event | category | flops | bytes accessed | tf_op | source)
XLA Modules:
  0.0 43.4 jit_solution(2870115414265204746)
XLA Ops:
  1.3 37.8 %shard_map.144 = (bf16[1,4,4096]{2,1,0:T(4,128)(2,1)S(1)}, bf16[1,4,4096]{2,1,0:T(4,128)(2,1)S(1)}, bf16[1,4096,512]{2,1,0:T(8,128)(2,1)S(1)}, bf16[1,512,4096]{...) custom-call(bf16[1,256,4096]{2,1,0:T(8,128)(2,1)} %x_hbm.1, ...), custom_call_target="tpu_custom_call" | custom-call | flops 6442450944 | bytes 14680064 | tf_op jit(solution)/shard_map/pallas_call | solution.py:293
  39.1 4.3 %shard_map.145 = (bf16[1,4,4096]{2,1,0:T(4,128)(2,1)}, bf16[1,4,4096]{2,1,0:T(4,128)(2,1)}, bf16[1,4096,512]{2,1,0:T(8,128)(2,1)}, bf16[1,512,4096]{2,1,0:T(8,12...) custom-call(bf16[1,4,4096]{2,1,0:T(4,128)(2,1)S(1)} %get-tuple-element.14.refs_0_, ...), custom_call_target="tpu_custom_call" | custom-call | bytes 12582912 | tf_op jit(solution)/shard_map/pallas_call | solution.py:356

commit v6 on v5

--- a/solution.py
+++ b/solution.py
@@ -66,7 +66,8 @@
 
     barrier = pltpu.get_barrier_semaphore()
 
-    rotate(here, lambda k: pl.semaphore_signal(barrier, inc=1, device_id=in_plane(k), device_id_type=MESH))
+    for d in range(1, 16):
+        pl.semaphore_signal(barrier, inc=1, device_id=in_plane((here + d) % 16), device_id_type=MESH)
     for d in (1, 2, 3):
         pl.semaphore_signal(barrier, inc=1, device_id=on_ring((ring + d) % 4), device_id_type=MESH)
     pl.semaphore_signal(barrier, inc=1, device_id=(1 - rep, f), device_id_type=MESH)
@@ -196,9 +197,9 @@
                     for act in acts:
                         act(core, e)
 
-    def third(n):
+    def third(*sums):
         slot = c * 8 + plane * 2 + z
-        for e in FAR:
+        for e, n in ((e, n) for e in FAR for n in sums):
             q = block_of(e)
             got = r1.at[n, :, q]
             remote(got, got, sr.at[n], qr.at[n, e], peer).wait_recv()
@@ -209,7 +210,8 @@
             for i in (2, 3, 0, 1) if e else (2, 3, 1):
                 k = 4 * q + (z * 2 + c + i) % 4
                 remote(sp.at[n, k], rp.at[n, slot], s2.at[n], q2.at[n], in_plane(k)).start()
-        rp[n, slot] = sp[n, here]
+        for n in sums:
+            rp[n, slot] = sp[n, here]
 
     def third_all(n):
         return remote(sp.at[n, pl.ds(0, 15)], rp.at[n, pl.ds(0, 15)], s2.at[n], q2.at[n], peer)
@@ -252,8 +254,7 @@
 
     dg_ref[0] = dot(hid[...], cotg[...].reshape(256, 4096), 0, 0).astype(BF)
     ug_ref[0] = dot(x_v[...], pg[...], 0, 0).astype(BF)
-    third(0)
-    third(1)
+    third(0, 1)
 
     loads[5].wait()
     loads[6].wait()

time: 43.6 us -> 43.4 us (level)
  no operation moved by 1% of the time
where the time goes in v6:
time: 43.4 us; the launch traced here: 43.3 us
  Pallas kernels  42 us (97%)
  between operations  1.29 us (3%)
    pallas_call x1, Pallas kernels, step_call(): pl.pallas_call(step_kernel, out_shape=(pltpu.VMEM((1, 4, 4096), BF), pltp...  37.7 us
    pallas_call x1, Pallas kernels, write_call(): pl.pallas_call(write_kernel, out_shape=tuple((jax.ShapeDtypeStruct(a.shap...  4.33 us

profile of v6, /device:TPU:1, one launch (start us, length us, event | category | flops | bytes accessed | tf_op | source)
XLA Modules:
  0.0 43.3 jit_solution(11123285355062238963)
XLA Ops:
  1.3 37.7 %shard_map.144 = (bf16[1,4,4096]{2,1,0:T(4,128)(2,1)S(1)}, bf16[1,4,4096]{2,1,0:T(4,128)(2,1)S(1)}, bf16[1,4096,512]{2,1,0:T(8,128)(2,1)S(1)}, bf16[1,512,4096]{...) custom-call(bf16[1,256,4096]{2,1,0:T(8,128)(2,1)} %x_hbm.1, ...), custom_call_target="tpu_custom_call" | custom-call | flops 6442450944 | bytes 14680064 | tf_op jit(solution)/shard_map/pallas_call | solution.py:294
  39.0 4.3 %shard_map.145 = (bf16[1,4,4096]{2,1,0:T(4,128)(2,1)}, bf16[1,4,4096]{2,1,0:T(4,128)(2,1)}, bf16[1,4096,512]{2,1,0:T(8,128)(2,1)}, bf16[1,512,4096]{2,1,0:T(8,12...) custom-call(bf16[1,4,4096]{2,1,0:T(4,128)(2,1)S(1)} %get-tuple-element.14.refs_0_, ...), custom_call_target="tpu_custom_call" | custom-call | bytes 12582912 | tf_op jit(solution)/shard_map/pallas_call | solution.py:357
